TPU v7x, 512 devices: a whole 4x4x16 slice. The times are simulated.
512 devices in a mesh: dp: 32 (over y_hi, z), ctx: 16 (over y_lo, x, core).
Axes of the slice: x: 4, y: 4 (y_hi: 2, y_lo: 2; y = y_hi * 2 + y_lo), z: 16, core: 2. Of those that a mesh axis runs over, the one named last changes fastest.
Arguments:
- bases: int32 [32, 163840], P('dp', 'ctx'), may hold values from 0 to 3
- embed_w: bfloat16 [512, 1536], replicated, may hold values from -0.5 to 0.5
- conv_w: bfloat16 [5, 1536, 1536], P(None, None, 'ctx'), may hold values from -0.0625 to 0.0625
- conv_b: float32 [1536], P('ctx'), may hold values from -3 to 3
- norm_g: float32 [1536], replicated, may hold values from 0.1 to 1.9
- qkv_w: bfloat16 [1536, 3072], P(None, 'ctx'), may hold values from -1 to 1
- wo: bfloat16 [1024, 1536], P('ctx'), may hold values from -1.5 to 1.5
- cotangent: bfloat16 [32, 1280, 1536], P('dp', 'ctx'), may hold values from -0.59765625 to 0.59765625
Outputs:
- layer_out: bfloat16 [32, 1280, 1536], P('dp', 'ctx')
- wo_grad: bfloat16 [1024, 1536], P('ctx')
All inputs are finite; a program needn't handle non-finite values.
Results may differ from a plain program's by a relative error of at most 0.024.
Values may be sent and summed in bfloat16 or wider, within the bound.
A program may use at most 64 MiB of HBM per device.

v0:
```python
import jax
import jax.numpy as jnp
from jax import lax
from jax.sharding import PartitionSpec as P

KW = 5
PATCH = 128


def patch_embed(seq_bases, embed_w):
    grouped = seq_bases.reshape(-1, PATCH)
    onehot = (grouped[:, :, None] == jnp.arange(4, dtype=jnp.int32)[None, None, :]).astype(
        jnp.bfloat16
    )
    onehot = onehot.reshape(grouped.shape[0], PATCH * 4)
    return jnp.dot(onehot, embed_w, preferred_element_type=jnp.float32).astype(jnp.bfloat16)


def conv_section(embedded, residual, conv_w, conv_b):
    half_kernel = KW // 2
    seq_rows = embedded.shape[0]
    padded = jnp.pad(embedded, ((half_kernel, half_kernel), (0, 0)))
    pre_act = jnp.zeros((seq_rows, conv_w.shape[2]), jnp.float32) + conv_b[None, :]
    for tap_index in range(KW):
        pre_act = pre_act + jnp.dot(
            padded[tap_index : tap_index + seq_rows],
            conv_w[tap_index],
            preferred_element_type=jnp.float32,
        )
    return (residual.astype(jnp.float32) + jax.nn.gelu(pre_act)).astype(jnp.bfloat16)


def rms_norm(stream, norm_g):
    values = stream.astype(jnp.float32)
    rescale = lax.rsqrt(jnp.mean(values * values, axis=-1, keepdims=True) + 1e-06)
    return (values * rescale * norm_g[None, :]).astype(jnp.bfloat16)


def attend(head_proj, head_size):
    query_rows = head_proj[:, :head_size]
    key_rows = head_proj[:, head_size : 2 * head_size]
    value_rows = head_proj[:, 2 * head_size :]
    scores = jnp.dot(query_rows, key_rows.T, preferred_element_type=jnp.float32) * head_size ** (
        -0.5
    )
    row_peak = jnp.max(scores, axis=1, keepdims=True)
    exponent = jnp.exp(scores - row_peak)
    weights = (exponent / jnp.sum(exponent, axis=1, keepdims=True)).astype(jnp.bfloat16)
    return jnp.dot(weights, value_rows, preferred_element_type=jnp.float32).astype(jnp.bfloat16)


def per_device(bases, embed_w, conv_w, conv_b, norm_g, qkv_w, wo, cotangent):
    own_index = lax.axis_index("ctx")
    block_cols = conv_w.shape[2]
    head_size = wo.shape[0]
    embedded = lax.all_gather(patch_embed(bases[0], embed_w), "ctx", axis=0, tiled=True)
    residual = lax.dynamic_slice_in_dim(embedded, own_index * block_cols, block_cols, 1)
    stream_block = conv_section(embedded, residual, conv_w, conv_b)
    stream_own = lax.all_to_all(stream_block, "ctx", split_axis=0, concat_axis=1, tiled=True)
    projected = jnp.dot(
        lax.all_gather(rms_norm(stream_own, norm_g), "ctx", axis=0, tiled=True),
        qkv_w,
        preferred_element_type=jnp.float32,
    )
    attended = attend(projected.astype(jnp.bfloat16), head_size)
    chosen = attended
    summed = lax.psum_scatter(
        jnp.dot(chosen, wo, preferred_element_type=jnp.float32).astype(jnp.bfloat16),
        "ctx",
        scatter_dimension=0,
        tiled=True,
    ).astype(jnp.float32)
    layer_out = (stream_own.astype(jnp.float32) + summed).astype(jnp.bfloat16)[None]
    chosen = attended
    local_grad = lax.dot_general(
        chosen,
        lax.all_gather(cotangent[0], "ctx", axis=0, tiled=True),
        (((0,), (0,)), ((), ())),
        preferred_element_type=jnp.float32,
    )
    grad_sum = lax.psum(local_grad, "dp")
    return (layer_out, grad_sum.astype(jnp.bfloat16))


def solution(mesh):
    return jax.shard_map(
        per_device,
        mesh=mesh,
        in_specs=(
            P("dp", "ctx"),
            P(),
            P(None, None, "ctx"),
            P("ctx"),
            P(),
            P(None, "ctx"),
            P("ctx", None),
            P("dp", "ctx", None),
        ),
        out_specs=(P("dp", "ctx", None), P("ctx", None)),
        check_vma=False,
    )
```

profile of v0, /device:TPU:6, one launch (start us, length us, event | category | flops | bytes accessed | tf_op | source)
XLA Modules:
  0.0 338.3 jit_solution(4462944720606357154)
XLA Ops:
  7.2 1.0 copy.30
  8.6 1.2 convolution_convert_fusion.2
  9.9 49.1 %all-gather.5.cloned.1.call-done = bf16[1280,1536]{1,0:T(8,128)(2,1)} async-done(((bf16[80,1536]{1,0:T(8,128)(2,1)}), bf16[1280,1536]{1,0:T(8,128)(2,1)}) %all-gather.5.cloned.1.call-update) | async-done | bytes 3932176 | tf_op jit(solution)/shard_map/all_gather | solution.py:56
  59.0 1.2 constant_dynamic-slice_fusion
  60.4 3.6 %fusion.7 = f32[1280,96]{0,1:T(8,128)S(1)} fusion(bf16[1280,1536]{1,0:T(8,128)(2,1)} %all-gather.5.cloned.1.call-done, bf16[5,1536,96]{1,2,0:T(8,128)(2,1)} %param.10), kind=kOutput, calls=%fused_computation.11 | convolution fusion | flops 377487360 | bytes 4718592 | tf_op jit(solution)/shard_map/dot_general | solution.py:25
  64.3 1.3 fusion.3
  65.6 1.3 fusion.5
  66.9 1.4 fusion.21
  68.3 1.4 fusion.34
  70.0 11.1 %all_to_all.13 = bf16[16,80,96]{2,1,0:T(8,128)(2,1)S(1)} all-to-all(bf16[16,80,96]{2,1,0:T(8,128)(2,1)S(1)} %bitcast.32), channel_id=1, replica_groups=mesh['dp'=32,'ctx'=16] {'ctx'}, dimensions={0} | all-to-all | bytes 491520 | tf_op jit(solution)/shard_map/all_to_all | solution.py:59
  81.3 0.3 reshape.25
  81.8 0.8 multiply_convert_fusion
  82.7 0.7 all-gather.9.cloned.1.call-update
  83.4 0.2 reduce-scatter.2.cloned.1.call-start
  83.6 44.0 %all-gather.7.cloned.1.call-done = bf16[1280,1536]{1,0:T(8,128)(2,1)} async-done(((bf16[80,1536]{1,0:T(8,128)(2,1)}), bf16[1280,1536]{1,0:T(8,128)(2,1)}) %all-gather.7.cloned.1.call-update) | async-done | bytes 3932176 | tf_op jit(solution)/shard_map/all_gather | solution.py:61
  127.6 3.7 %convolution_convert_fusion.1 = bf16[1280,192]{0,1:T(8,128)(2,1)S(1)} fusion(bf16[1280,1536]{1,0:T(8,128)(2,1)} %all-gather.7.cloned.1.call-done, bf16[1536,192]{0,1:T(8,128)(2,1)} %param.13), kind=kOutput, calls=%fused_computation.20 | convolution fusion | flops 755220480 | bytes 5013504 | tf_op jit(solution)/shard_map/dot_general | solution.py:60
  131.2 1.1 fusion.55
  132.3 1.0 fusion
  133.3 1.2 fusion.24
  134.5 3.1 convolution_convert_fusion
  137.6 36.8 %all-gather.9.cloned.1.call-done = bf16[1,1280,1536]{2,1,0:T(8,128)(2,1)} async-done(((bf16[1,80,1536]{2,1,0:T(8,128)(2,1)}), bf16[1,1280,1536]{2,1,0:T(8,128)(2,1)}) %all-gather.9.cloned.1.call-update) | async-done | bytes 3932176 | tf_op jit(solution)/shard_map/all_gather | solution.py:77
  174.4 2.9 fusion.1
  177.3 152.8 %all-reduce.2 = bf16[64,1536]{1,0:T(8,128)(2,1)} all-reduce(f32[64,1536]{1,0:T(8,128)S(1)} %fusion.1), channel_id=1, replica_groups=mesh['dp'=32,'ctx'=16] {'dp'}, use_global_device_ids=true, to_apply=%region_4.5 | all-reduce | flops 98304 | bytes 589824 | tf_op jit(solution)/shard_map/psum | solution.py:81
  330.1 1.7 fusion.46
  (28 shorter events, 1.6 us)
Async XLA Ops:
  7.2 1.4 copy-start
  7.2 51.8 %all-gather.5.cloned.1.call-start = ((), (), s32[]{:S(2)}) async-start(), calls=%async_computation.2 | async-start | bytes 4177920 | tf_op jit(solution)/shard_map/all_gather | solution.py:56
  9.8 117.7 %all-gather.7.cloned.1.call-start = ((), (), s32[]{:S(2)}) async-start(), calls=%async_computation.3 | async-start | bytes 4177920 | tf_op jit(solution)/shard_map/all_gather | solution.py:61
  60.4 3.7 %copy-start.1 = (bf16[1280,1536]{1,0:T(8,128)(2,1)S(1)}, bf16[1280,1536]{1,0:T(8,128)(2,1)}, u32[]{:S(2)}) copy-start(bf16[1280,1536]{1,0:T(8,128)(2,1)} %all-gather.5.cloned.1.call-done) | copy-start | bytes 11796484
  60.4 3.8 %copy-start.3 = (bf16[5,1536,96]{1,2,0:T(8,128)(2,1)S(1)}, bf16[5,1536,96]{1,2,0:T(8,128)(2,1)}, u32[]{:S(2)}) copy-start(bf16[5,1536,96]{1,2,0:T(8,128)(2,1)} %param.10) | copy-start | bytes 4423684
  65.6 1.3 copy-start.5
  69.7 12.1 %copy-start.4 = (f32[1536]{0:T(1024)S(1)}, f32[1536]{0:T(1024)}, u32[]{:S(2)}) copy-start(f32[1536]{0:T(1024)} %param.12) | copy-start | bytes 18436
  82.7 91.7 %all-gather.9.cloned.1.call-start = ((), (), s32[]{:S(2)}) async-start(), calls=%async_computation.5 | async-start | bytes 4177920 | tf_op jit(solution)/shard_map/all_gather | solution.py:77
  83.4 246.7 %reduce-scatter.2.cloned.1.call-start = ((), (), s32[]{:S(2)}) async-start(), calls=%async_computation.4 | async-start | bytes 4177920 | tf_op jit(solution)/shard_map/reduce_scatter | solution.py:67
  133.3 1.2 copy-start.2
Sparse Core Ops, SparseCore 0:
  10.7 48.2 all-gather.4
  82.8 44.7 all-gather.6
  129.7 44.6 all-gather.8
  177.1 71.7 reduce-scatter.1
where the time goes:
time: 339 us; the launch traced here: 338 us
  blocking collectives  164 us (48%)
  waiting for transfers between devices  131 us (39%)
  matrix products  22.2 us (7%)
  between operations  13.9 us (4%)
  other arithmetic  3.69 us (1%)
  local copies, waits for them, and re-layouts  3.66 us (1%)
    psum x1, blocking collectives, per_device(): grad_sum = lax.psum(local_grad, 'dp')  153 us
    all_gather x1, waiting for transfers between devices, per_device(): lax.all_gather(patch_embed(bases[0], embed_w), 'ctx', axis=0, tiled=True)  49.1 us
    all_gather x1, waiting for transfers between devices, per_device(): lax.all_gather(rms_norm(stream_own, norm_g), 'ctx', axis=0, tiled=True)  44 us
    all_gather x1, waiting for transfers between devices, per_device(): lax.all_gather(cotangent[0], 'ctx', axis=0, tiled=True)  36.8 us
    all_to_all x1, blocking collectives, per_device(): lax.all_to_all(stream_block, 'ctx', split_axis=0, concat_axis=1, tiled=True)  11.1 us
    dot_general x5, matrix products, conv_section(): jnp.dot(padded[tap_index:tap_index + seq_rows], conv_w[tap_index], prefer...  9.06 us
  transfers between devices with their start and end apart: 4, of which 3 were waited for; matrix products, arithmetic and copies ran while one was open for 4% of the time, Pallas kernels for 0%

commit v1 on v0

v1 whole, which is shorter than its diff:
```python
import functools

import jax
import jax.numpy as jnp
from jax import lax
from jax.experimental import pallas as pl
from jax.experimental.pallas import tpu as pltpu
from jax.sharding import PartitionSpec as P

MESH = pl.DeviceIdType.MESH
BF = jnp.bfloat16
F32 = jnp.float32
LA = 384


def _al(v, m):
    return pl.multiple_of(v, m)


def _dot(a, b):
    return jnp.dot(a, b, preferred_element_type=F32)


def _gelu(v):
    return 0.5 * v * (1.0 + jnp.tanh(0.7978845608028654 * (v + 0.044715 * (v * v * v))))


def front_kernel(
    bases_ref, embed_ref, convw_ref, convb_ref, wt_ref, cot_ref,
    grad_ref, aown_ref, sown_ref,
    bsend, ball, wcat, wc, wcp, oh, yb, st, xt, wt, qt, kv, ks, at, an, ath, aown, sbuf, sown, cotr,
    ss_b, rs_b, ss_w, rs_w, ss1, rs1, ss2, rs2, ss_c, rs_c, ss_k, rs_k, ss_s, rs_s, ss_t, rs_t, ss_a, rs_a,
    ss_d, rs_d,
):
    me = lax.axis_index("ctx")
    core = lax.rem(me, 2)
    x = lax.rem(me // 2, 4)
    y = me // 8
    chip = me // 2
    sib = me + 1 - 2 * core

    def ctx(yy, xx, cc):
        return (yy * 4 + lax.rem(xx, 4)) * 2 + cc

    def rcopy(src, dst, ssem, rsem, to):
        return pltpu.make_async_remote_copy(
            src_ref=src, dst_ref=dst, send_sem=ssem, recv_sem=rsem,
            device_id={"ctx": to}, device_id_type=MESH,
        )

    barrier = pltpu.get_barrier_semaphore()
    for d in range(1, 16):
        pl.semaphore_signal(barrier, inc=1, device_id={"ctx": lax.rem(me + d, 16)}, device_id_type=MESH)
    mine = bases_ref[...].astype(F32).astype(BF)
    bsend[...] = mine
    ball[pl.ds(_al(me * 80, 16), 80), :] = mine
    pl.semaphore_wait(barrier, 15)

    def bcopy(d):
        return rcopy(bsend, ball.at[pl.ds(_al(me * 80, 16), 80)], ss_b.at[d - 1], rs_b.at[d - 1], lax.rem(me + d, 16))

    def start_b(d, c):
        bcopy(d).start()
        return c

    lax.fori_loop(1, 16, start_b, 0)
    wcopy = rcopy(wt_ref, wt.at[pl.ds(_al(core * 192, 16), 192)], ss_w, rs_w, sib)
    wcopy.start()
    wt[pl.ds(_al(core * 192, 16), 192), :] = wt_ref[...]

    def fill(i, c):
        rows = pl.ds(_al(i * 256, 256), 256)
        for j in range(5):
            wcat[rows, 128 * j : 128 * j + 128] = jnp.zeros((256, 128), BF)
            wcat[rows, 128 * j : 128 * j + 96] = convw_ref[j, rows, :]
        r = lax.broadcasted_iota(jnp.int32, (256, 128), 0) + i * 256
        cc = lax.broadcasted_iota(jnp.int32, (256, 128), 1)
        pick = jnp.where(jnp.logical_and(r == cc + 96 * me, cc < 96), 1.0, 0.0)
        wcat[rows, 640:768] = pick.astype(BF)
        return c

    lax.fori_loop(0, 6, fill, 0)

    def comp(i, c):
        cols = pl.ds(_al(i * 256, 256), 256)
        prod = _dot(embed_ref[...], wcat[:, cols])
        wc[2 * i] = prod[:, 0:128]
        wc[2 * i + 1] = prod[:, 128:256]
        return c

    lax.fori_loop(0, 3, comp, 0)
    for b in range(4):
        for j in range(6):
            wcp[128 * b : 128 * b + 128, 128 * j : 128 * j + 128] = wc[j, pl.ds(b, 128, stride=4), :].astype(BF)
    yb[0:8, :] = jnp.zeros((8, 768), F32)
    yb[1288:1296, :] = jnp.zeros((8, 768), F32)

    def wait_b(d, c):
        bcopy(d).wait_recv()
        return c

    lax.fori_loop(1, 16, wait_b, 0)

    def taps(i, c):
        rows = pl.ds(_al(i * 256, 256), 256)
        bb = ball[rows, :].astype(F32)
        for b in range(4):
            oh[:, 128 * b : 128 * b + 128] = jnp.where(bb == float(b), 1.0, 0.0).astype(BF)
        yb[pl.ds(_al(i * 256 + 8, 8), 256), :] = _dot(oh[...], wcp[...])
        return c

    lax.fori_loop(0, 5, taps, 0)

    def act(q, c):
        win = pl.ds(_al(q * 128, 8), 144)
        pre = jnp.zeros((128, 128), F32) + convb_ref[...]
        for j in range(5):
            pre = pre + yb[win, 128 * j : 128 * j + 128][6 + j : 134 + j]
        val = yb[pl.ds(_al(q * 128 + 8, 8), 128), 640:768] + _gelu(pre)
        st[q // 5, :, pl.ds(_al(lax.rem(q, 5) * 128, 128), 128)] = val.T[0:96, :].astype(BF)
        return c

    own_rows = pl.ds(_al(me * 96, 16), 96)
    sends = []

    def s1(rel, ct):
        to = ctx(y, x + rel + 1, ct) if rel < 3 else ctx(1 - y, x, ct)
        return rcopy(st.at[ct], xt.at[own_rows], ss1.at[rel * 2 + ct], rs1.at[rel * 2 + core], to)

    for half in range(2):
        lax.fori_loop(5 * half, 5 * half + 5, act, 0)
        for rel in (3, 0, 2, 1):
            cp = s1(rel, half)
            cp.start()
            sends.append(cp)

        @pl.when(core == half)
        def _():
            xt[own_rows, :] = st[half]

        @pl.when(core != half)
        def _():
            rcopy(st.at[half], xt.at[own_rows], ss1.at[8], rs1.at[8], sib).start()

    def chip_rows(kk):
        return pl.ds(_al(kk * 192, 16), 192)

    def s1_wait(rel):
        for cs in range(2):
            rcopy(st.at[0], xt.at[own_rows], ss1.at[rel * 2 + cs], rs1.at[rel * 2 + cs], sib).wait_recv()

    s1_wait(3)
    ky = (1 - y) * 4 + x
    for d in (1, 3, 2):
        src = xt.at[chip_rows(ky), LA:640]
        cp = rcopy(src, src, ss2.at[2 + d], rs2.at[2 + d], ctx(y, x + d, core))
        cp.start()
        sends.append(cp)
    for d in (1, 3, 2):
        s1_wait(d - 1)
        src = xt.at[chip_rows(y * 4 + lax.rem(x + 4 - d, 4)), 0:LA]
        cp = rcopy(src, src, ss2.at[d - 1], rs2.at[d - 1], ctx(1 - y, x, core))
        cp.start()
        sends.append(cp)

    my_tok = pl.ds(_al(lax.rem(me, 8) * 80, 16), 80)
    cots = []
    for d in (1, 3, 2):
        for cc in range(2):
            cols = slice(768 * cc, 768 * cc + 768)
            cp = rcopy(cot_ref.at[:, cols], cotr.at[my_tok, cols], ss_c.at[2 * d - 2 + cc], rs_c.at[2 * d - 2 + core],
                       ctx(y, x + d, cc))
            cp.start()
            cots.append(cp)
    for cc in range(2):
        cols = slice(768 * cc, 768 * cc + 768)

        @pl.when(core == cc)
        def _():
            cotr[my_tok, cols] = cot_ref[:, cols]

        @pl.when(core != cc)
        def _():
            rcopy(cot_ref.at[:, cols], cotr.at[my_tok, cols], ss_c.at[6], rs_c.at[6], sib).start()

    wcopy.wait()
    rcopy(st.at[0], xt.at[own_rows], ss1.at[8], rs1.at[8], sib).wait_recv()
    for d in (1, 3, 2):
        src = xt.at[chip_rows(0), LA:640]
        rcopy(src, src, ss2.at[2 + d], rs2.at[2 + d], sib).wait_recv()
        src = xt.at[chip_rows(0), 0:LA]
        rcopy(src, src, ss2.at[d - 1], rs2.at[d - 1], sib).wait_recv()

    def sq(i, acc):
        v = xt[pl.ds(_al(i * 128, 128), 128), :].astype(F32)
        return acc + jnp.sum((v * v).reshape(16, 8, 640), axis=0)

    total = lax.fori_loop(0, 12, sq, jnp.zeros((8, 640), F32))
    scale = lax.rsqrt(jnp.sum(total, axis=0, keepdims=True) * (1.0 / 1536.0) + 1e-06)
    for h in range(2):
        pr = _dot(wt[192 * h : 192 * h + 192, :], xt[...]) * scale
        qt[h] = (pr[0:64] * 0.125).astype(BF)
        kv[core, h] = pr[64:192].astype(BF)
    kcopy = rcopy(kv.at[core], kv.at[core], ss_k, rs_k, sib)
    kcopy.start()

    scopy = rcopy(sbuf.at[1 - core], sown, ss_s, rs_s, sib)

    @pl.when(core == y)
    def _():
        r = lax.broadcasted_iota(jnp.int32, (160, 640), 0) + 160 * x
        cidx = lax.broadcasted_iota(jnp.int32, (160, 640), 1)
        pick = jnp.where(r == cidx, 1.0, 0.0).astype(BF)
        for n in range(6):
            part = lax.dot_general(pick, xt[256 * n : 256 * n + 256, :], (((1,), (1,)), ((), ())),
                                   preferred_element_type=F32).astype(BF)
            sbuf[0, :, 256 * n : 256 * n + 256] = part[0:80]
            sbuf[1, :, 256 * n : 256 * n + 256] = part[80:160]
        sown[...] = sbuf[core]
        scopy.start()

    kcopy.wait()
    for h in range(2):
        for half in range(2):
            ks[h, 640 * half : 640 * half + 640, :] = kv[half, h, 0:64, :].astype(F32).T.astype(BF)

    def attend(i, c):
        lanes = pl.ds(_al(i * 128, 128), 128)
        outs = []
        for h in range(2):
            s = _dot(ks[h], qt[h, :, lanes])
            p = jnp.exp(s - jnp.max(s, axis=0, keepdims=True))
            den = jnp.sum(p, axis=0, keepdims=True)
            pb = p.astype(BF)
            o = _dot(kv[0, h, 64:128, :], pb[0:640]) + _dot(kv[1, h, 64:128, :], pb[640:1280])
            outs.append(o / den)
        both = jnp.concatenate(outs, axis=0)
        at[:, lanes] = both.astype(BF)
        an[lanes, :] = both.T.astype(BF)
        return c

    lax.fori_loop(0, 5, attend, 0)

    kx = core * 4 + x

    def tcopy(cc):
        return rcopy(at.at[64 * cc : 64 * cc + 64], ath.at[pl.ds(_al(y * 64, 16), 64)], ss_t.at[cc], rs_t.at[y],
                     kx * 2 + cc)

    for cc in range(2):
        @pl.when(kx * 2 + cc == me)
        def _():
            ath[pl.ds(_al(y * 64, 16), 64), :] = at[64 * cc : 64 * cc + 64, :]

        @pl.when(kx * 2 + cc != me)
        def _():
            tcopy(cc).start()

    def acopy(j):
        return rcopy(an.at[80 * j : 80 * j + 80], aown.at[:, pl.ds(_al(chip * 128, 128), 128)], ss_a.at[j], rs_a.at[chip],
                     8 * core + j)

    for j in range(8):
        @pl.when(8 * core + j == me)
        def _():
            aown[:, pl.ds(_al(chip * 128, 128), 128)] = an[80 * j : 80 * j + 80, :]

        @pl.when(8 * core + j != me)
        def _():
            acopy(j).start()

    for d in (1, 3, 2):
        for cs in range(2):
            rcopy(cot_ref.at[:, 0:768], cotr.at[my_tok, 0:768], ss_c.at[2 * d - 2 + cs], rs_c.at[2 * d - 2 + cs],
                  sib).wait_recv()
    rcopy(cot_ref.at[:, 0:768], cotr.at[my_tok, 0:768], ss_c.at[6], rs_c.at[6], sib).wait_recv()
    half_cols = cotr.at[:, pl.ds(_al(core * 768, 128), 768)]
    dcopy = rcopy(half_cols, half_cols, ss_d, rs_d, sib)
    dcopy.start()

    def t_wait(slot):
        rcopy(at.at[0:64], ath.at[0:64], ss_t.at[0], rs_t.at[slot], sib).wait_recv()

    t_wait(1 - y)

    @pl.when(core != y)
    def _():
        t_wait(y)

    dcopy.wait()
    for n in range(3):
        cols = slice(512 * n, 512 * n + 512)
        grad_ref[:, cols] = _dot(ath[...], cotr[:, cols]).astype(BF)

    for k in range(8):
        @pl.when(2 * k + y != me)
        def _():
            rcopy(an.at[0:80], aown.at[:, 0:128], ss_a.at[0], rs_a.at[k], sib).wait_recv()

    @pl.when(core != y)
    def _():
        scopy.wait_recv()

    aown_ref[...] = aown[...]
    sown_ref[...] = sown[...]

    @pl.when(core == y)
    def _():
        scopy.wait_send()

    def send_b(d, c):
        bcopy(d).wait_send()
        return c

    lax.fori_loop(1, 16, send_b, 0)
    for cp in sends + cots:
        cp.wait_send()
    rcopy(st.at[0], xt.at[own_rows], ss1.at[8], rs1.at[8], sib).wait_send()
    rcopy(cot_ref.at[:, 0:768], cotr.at[my_tok, 0:768], ss_c.at[6], rs_c.at[6], sib).wait_send()
    for cc in range(2):
        @pl.when(kx * 2 + cc != me)
        def _():
            tcopy(cc).wait_send()
    for j in range(8):
        @pl.when(8 * core + j != me)
        def _():
            acopy(j).wait_send()


def grad_kernel(g_ref, out_ref, yr, zs, zr, fb, rc, ss_y, rs_y, ss_z, rs_z, ss_f, rs_f):
    dp = lax.axis_index("dp")
    me = lax.axis_index("ctx")
    yh, z = dp // 16, lax.rem(dp, 16)
    yl, rest = me // 8, lax.rem(me, 8)
    ring = 2 * yh + yl

    def rcopy(src, dst, ssem, rsem, to):
        return pltpu.make_async_remote_copy(
            src_ref=src, dst_ref=dst, send_sem=ssem, recv_sem=rsem, device_id=to, device_id_type=MESH
        )

    def ring_dev(e):
        r = lax.rem(ring + e, 4)
        return (r // 2) * 16 + z, lax.rem(r, 2) * 8 + rest

    barrier = pltpu.get_barrier_semaphore()

    def sig(d, c):
        pl.semaphore_signal(barrier, inc=1, device_id=(lax.rem(dp + d, 32), me), device_id_type=MESH)
        return c

    lax.fori_loop(1, 32, sig, 0)
    for e in (1, 3):
        pl.semaphore_signal(barrier, inc=1, device_id=ring_dev(e), device_id_type=MESH)
    pl.semaphore_wait(barrier, 33)

    def block(r):
        return pl.ds(_al(lax.rem(r, 2) * 64, 16), 64), pl.ds(_al((r // 2) * 768, 128), 768)

    ysend = []
    for e in (1, 2, 3):
        rows, cols = block(lax.rem(ring + e, 4))
        cp = rcopy(g_ref.at[rows, cols], yr.at[e - 1], ss_y.at[e - 1], rs_y.at[e - 1], ring_dev(e))
        cp.start()
        ysend.append(cp)
    rows, cols = block(ring)
    acc = g_ref[rows, cols].astype(F32)
    for e in (1, 3, 2):
        ysend[e - 1].wait_recv()
        acc = acc + yr[e - 1].astype(F32)
    zs[...] = acc.astype(BF)

    def zcopy(q):
        return rcopy(zs.at[16 * (q // 3) : 16 * (q // 3) + 16, 256 * (q % 3) : 256 * (q % 3) + 256], zr.at[z],
                     ss_z.at[q], rs_z.at[z], (yh * 16 + q, me))

    for q in range(12):
        @pl.when(z != q)
        def _():
            zcopy(q).start()

    zrows = pl.ds(_al((z // 3) * 16, 16), 16)
    zlane = lax.rem(z, 3) * 256

    def fcopy(d):
        return rcopy(rc, fb.at[zrows, pl.ds(_al(yh * 768 + zlane, 128), 256)], ss_f.at[d - 1], rs_f.at[yh * 12 + z],
                     (lax.rem(dp + d, 32), me))

    @pl.when(z < 12)
    def _():
        zr[z] = zs[zrows, pl.ds(_al(zlane, 128), 256)]

        def wait_z(s, c):
            @pl.when(s != z)
            def _():
                rcopy(rc, zr.at[s], ss_z.at[0], rs_z.at[s], (yh * 16 + s, me)).wait_recv()
            return c

        lax.fori_loop(0, 16, wait_z, 0)
        tot = zr[0].astype(F32)
        for s in range(1, 16):
            tot = tot + zr[s].astype(F32)
        rc[...] = tot.astype(BF)
        fb[zrows, pl.ds(_al(yh * 768 + zlane, 128), 256)] = tot.astype(BF)

        def start_f(d, c):
            fcopy(d).start()
            return c

        lax.fori_loop(1, 32, start_f, 0)

    def wait_f(s, c):
        @pl.when(s != yh * 12 + z + jnp.where(z < 12, 0, 1000))
        def _():
            rcopy(rc, fb.at[0:16, 0:256], ss_f.at[0], rs_f.at[s], (dp, me)).wait_recv()
        return c

    lax.fori_loop(0, 24, wait_f, 0)
    out_ref[...] = fb[...]
    for cp in ysend:
        cp.wait_send()
    for q in range(12):
        @pl.when(z != q)
        def _():
            zcopy(q).wait_send()

    @pl.when(z < 12)
    def _():
        def wait_s(d, c):
            fcopy(d).wait_send()
            return c

        lax.fori_loop(1, 32, wait_s, 0)


def per_device(bases, embed_w, conv_w, conv_b, norm_g, qkv_w, wo, cotangent):
    vm = pl.BlockSpec(memory_space=pltpu.VMEM)
    dma = pltpu.SemaphoreType.DMA
    wo_all = lax.all_gather(wo, "ctx", axis=0, tiled=True)
    wt = (qkv_w.T.astype(F32) * norm_g[None, :]).astype(BF)
    bias = jnp.pad(conv_b, (0, 32))[None]
    V = pltpu.VMEM
    grad, aown, sown = pl.pallas_call(
        front_kernel,
        out_shape=(
            jax.ShapeDtypeStruct((128, 1536), BF),
            jax.ShapeDtypeStruct((80, 1024), BF),
            jax.ShapeDtypeStruct((80, 1536), BF),
        ),
        in_specs=[vm] * 6,
        out_specs=(vm,) * 3,
        scratch_shapes=[
            V((80, 128), BF), V((1280, 128), BF), V((1536, 768), BF), V((6, 512, 128), F32), V((512, 768), BF),
            V((256, 512), BF), V((1296, 768), F32), V((2, 96, 640), BF), V((1536, 640), BF), V((384, 1536), BF),
            V((2, 64, 640), BF), V((2, 2, 128, 640), BF), V((2, 1280, 64), BF), V((128, 640), BF), V((640, 128), BF),
            V((128, 640), BF), V((80, 1024), BF), V((2, 80, 1536), BF), V((80, 1536), BF), V((640, 1536), BF),
            dma((15,)), dma((15,)), dma, dma, dma((9,)), dma((9,)), dma((6,)), dma((6,)), dma((7,)), dma((7,)),
            dma, dma, dma, dma, dma((2,)), dma((2,)), dma((8,)), dma((8,)), dma, dma,
        ],
        compiler_params=pltpu.CompilerParams(collective_id=0, has_side_effects=True, vmem_limit_bytes=56 << 20),
        name="front",
    )(bases.reshape(80, 128), embed_w, conv_w, bias, wt, cotangent[0])
    wo_grad = pl.pallas_call(
        grad_kernel,
        out_shape=jax.ShapeDtypeStruct((64, 1536), BF),
        in_specs=[vm],
        out_specs=vm,
        scratch_shapes=[
            V((3, 64, 768), BF), V((64, 768), BF), V((16, 16, 256), BF), V((64, 1536), BF), V((16, 256), BF),
            dma((3,)), dma((3,)), dma((12,)), dma((16,)), dma((31,)), dma((24,)),
        ],
        compiler_params=pltpu.CompilerParams(collective_id=1, has_side_effects=True, vmem_limit_bytes=20 << 20),
        name="gradsum",
    )(grad)
    layer_out = (sown.astype(F32) + _dot(aown, wo_all)).astype(BF)[None]
    return layer_out, wo_grad


def solution(mesh):
    return jax.shard_map(
        per_device,
        mesh=mesh,
        in_specs=(
            P("dp", "ctx"), P(), P(None, None, "ctx"), P("ctx"), P(), P(None, "ctx"), P("ctx", None),
            P("dp", "ctx", None),
        ),
        out_specs=(P("dp", "ctx", None), P("ctx", None)),
        check_vma=False,
    )
```

time: 339 us -> 136 us (0.40)
  the two profiles are of different devices: /device:TPU:6 before, /device:TPU:1 now
where the time goes in v1:
time: 136 us; the launch traced here: 134 us
  Pallas kernels  109 us (80%)
  between operations  14.1 us (10%)
  local copies, waits for them, and re-layouts  5.96 us (4%)
  matrix products  3.3 us (2%)
    pallas_call x1, Pallas kernels, per_device(): pl.pallas_call(front_kernel, out_shape=(jax.ShapeDtypeStruct((128, 1536),...  67.5 us
    pallas_call x1, Pallas kernels, per_device(): pl.pallas_call(grad_kernel, out_shape=jax.ShapeDtypeStruct((64, 1536), BF...  41 us
    unnamed x10, local copies, waits for them, and re-layouts  5.45 us
    dot_general x1, matrix products, _dot(): return jnp.dot(a, b, preferred_element_type=F32)  3.3 us
  transfers between devices with their start and end apart: 1, of which 0 were waited for; matrix products, arithmetic and copies ran while one was open for 4% of the time, Pallas kernels for 81%

profile of v1, /device:TPU:1, one launch (start us, length us, event | category | flops | bytes accessed | tf_op | source)
XLA Modules:
  0.0 133.6 jit_solution(11648021079577847101)
XLA Ops:
  7.2 0.0 copy-start.3
  7.2 0.0 copy-start.2
  7.2 0.0 copy-start.1
  7.2 0.0 all-gather.2.cloned.1.call-start
  7.2 0.7 all-gather.2.cloned.1.call-update
  7.9 3.8 %copy.10.convw_ref = bf16[5,1536,96]{2,1,0:T(8,128)(2,1)} copy(bf16[5,1536,96]{1,2,0:T(8,128)(2,1)} %param.10) | data formatting | bytes 2949120 | tf_op args[2]
  11.7 0.0 copy-done.3
  11.7 0.5 pad_bitcast_fusion.convb_ref
  12.2 0.0 copy-done.2
  12.2 0.0 copy-done.1
  12.2 0.9 fusion.2.wt_ref
  13.2 67.5 %front.1 = (bf16[128,1536]{1,0:T(8,128)(2,1)}, bf16[80,1024]{1,0:T(8,128)(2,1)}, bf16[80,1536]{1,0:T(8,128)(2,1)}) custom-call(s32[80,128]{1,0:T(8,128)} %bitcast.11, bf16[512,1536]{1,0:T(8,128)(2,1)} %embed_ref.1, bf16[5,1536,96]{2,1,0:T(8,128)(2,1)} %copy.10.convw_ref, f32[1,128]{1,0:T(1,128)} %pad_bitcast_fusion.convb_ref, ...), custom_call_target="tpu_custom_call" | custom-call | tf_op jit(solution)/shard_map/front/pallas_call | solution.py:443
  80.7 0.0 copy-start
  80.7 1.0 copy-done
  81.7 41.0 %gradsum.1 = bf16[64,1536]{1,0:T(8,128)(2,1)S(1)} custom-call(bf16[128,1536]{1,0:T(8,128)(2,1)S(1)} %copy-done), custom_call_target="tpu_custom_call" | custom-call | tf_op jit(solution)/shard_map/gradsum/pallas_call | solution.py:463
  122.7 0.0 all-gather.2.cloned.1.call-done
  122.8 3.3 %fusion.1 = bf16[1,80,1536]{2,1,0:T(8,128)(2,1)} fusion(bf16[80,1024]{1,0:T(8,128)(2,1)} %get-tuple-element.6, bf16[1024,1536]{1,0:T(8,128)(2,1)} %all-gather.2.cloned.1.call-done, bf16[80,1536]{1,0:T(8,128)(2,1)} %get-tuple-element.5), kind=kOutput, calls=%fused_computation.2 | convolution fusion | flops 252026880 | bytes 3801088 | tf_op jit(solution)/shard_map/dot_general | solution.py:21
  126.1 0.7 copy.12
Async XLA Ops:
  7.2 4.5 %copy-start.3 = (f32[96]{0:T(128)S(1)}, f32[96]{0:T(128)}, u32[]{:S(2)}) copy-start(f32[96]{0:T(128)} %param.11) | copy-start | bytes 1156
  7.2 5.0 %copy-start.2 = (f32[1536]{0:T(1024)S(1)}, f32[1536]{0:T(1024)}, u32[]{:S(2)}) copy-start(f32[1536]{0:T(1024)} %param.12) | copy-start | bytes 18436
  7.2 5.0 %copy-start.1 = (bf16[1536,192]{0,1:T(8,128)(2,1)S(1)}, bf16[1536,192]{0,1:T(8,128)(2,1)}, u32[]{:S(2)}) copy-start(bf16[1536,192]{0,1:T(8,128)(2,1)} %param.13) | copy-start | bytes 1769476
  7.2 115.6 %all-gather.2.cloned.1.call-start = ((), (), s32[]{:S(2)}) async-start(), calls=%async_computation | async-start | bytes 3342336 | tf_op jit(solution)/shard_map/all_gather | solution.py:439
  80.7 1.0 copy-start
Sparse Core Ops, SparseCore 0:
  10.2 61.9 all-gather.1

commit v2 on v1

v2 whole, which is shorter than its diff:
```python
import functools

import jax
import jax.numpy as jnp
from jax import lax
from jax.experimental import pallas as pl
from jax.experimental.pallas import tpu as pltpu
from jax.sharding import PartitionSpec as P

MESH = pl.DeviceIdType.MESH
BF = jnp.bfloat16
F32 = jnp.float32
LA = 384


def _al(v, m):
    return pl.multiple_of(v, m)


def _dot(a, b):
    return jnp.dot(a, b, preferred_element_type=F32)


def _gelu(v):
    return 0.5 * v * (1.0 + jnp.tanh(0.7978845608028654 * (v + 0.044715 * (v * v * v))))


def layer_kernel(
    bases_ref, embed_ref, convt_ref, convb_ref, qkvt_ref, gain_ref, wo_ref, cot_ref,
    out_ref, grad_ref,
    bsend, ball, wcat, wc, wcp, oh, yb, st, xt, wt, qt, kv, ks, sc, at, an, ath, aown, sbuf, sown, cotr, wof,
    gl, yr, zs, nr, fr, rc, fb,
    ss_b, rs_b, ss_w, rs_w, ss1, rs1, ss2, rs2, ss_c, rs_c, ss_k, rs_k, ss_s, rs_s, ss_t, rs_t, ss_a, rs_a,
    ss_d, rs_d, ss_o, rs_o, ss_p, rs_p, ss_q, rs_q, ss_y, rs_y, ss_n, rs_n, ss_f, rs_f, ss_g, rs_g,
):
    dp = lax.axis_index("dp")
    me = lax.axis_index("ctx")
    yh, z = dp // 16, lax.rem(dp, 16)
    za, zb = z // 4, lax.rem(z, 4)
    core = lax.rem(me, 2)
    chip = me // 2
    x = lax.rem(chip, 4)
    y = me // 8
    sib = me + 1 - 2 * core
    ring = 2 * yh + y

    def ctx(yy, xx, cc):
        return (yy * 4 + lax.rem(xx, 4)) * 2 + cc

    def rcopy(src, dst, ssem, rsem, to):
        return pltpu.make_async_remote_copy(
            src_ref=src, dst_ref=dst, send_sem=ssem, recv_sem=rsem,
            device_id=to if isinstance(to, tuple) else (dp, to), device_id_type=MESH,
        )

    def ring_dev(e):
        r = lax.rem(ring + e, 4)
        return (r // 2) * 16 + z, lax.rem(r, 2) * 8 + lax.rem(me, 8)

    def near(e):
        return yh * 16 + za * 4 + lax.rem(zb + e, 4), me

    def across(e):
        return (1 - yh) * 16 + za * 4 + lax.rem(zb + e, 4), me

    def far(e):
        return yh * 16 + lax.rem(za + e, 4) * 4 + zb, me

    barrier = pltpu.get_barrier_semaphore()
    greet = [(dp, lax.rem(me + d, 16)) for d in range(1, 16)]
    greet += [near(e) for e in (1, 2, 3)] + [far(e) for e in (1, 2, 3)] + [across(e) for e in range(4)]
    greet += [((1 - yh) * 16 + z, (1 - y) * 8 + lax.rem(me, 8))]
    for to in greet:
        pl.semaphore_signal(barrier, inc=1, device_id=to, device_id_type=MESH)
    mine = bases_ref[...].astype(F32).astype(BF)
    bsend[...] = mine
    ball[pl.ds(_al(me * 80, 16), 80), :] = mine
    wrows = pl.ds(_al(core * 192, 16), 192)
    wt[wrows, :] = (qkvt_ref[...].astype(F32) * gain_ref[...]).astype(BF)
    pl.semaphore_wait(barrier, len(greet))

    def bcopy(d):
        return rcopy(bsend, ball.at[pl.ds(_al(me * 80, 16), 80)], ss_b.at[d - 1], rs_b.at[d - 1], lax.rem(me + d, 16))

    def start_b(d, c):
        bcopy(d).start()
        return c

    lax.fori_loop(1, 16, start_b, 0)
    wcopy = rcopy(wt.at[wrows], wt.at[wrows], ss_w, rs_w, sib)
    wcopy.start()
    sends = []

    wo_rows = pl.ds(_al(me * 64, 16), 64)
    for d in (1, 3, 2):
        for cc in range(2):
            cols = slice(768 * cc, 768 * cc + 768)
            cp = rcopy(wo_ref.at[:, cols], wof.at[wo_rows, cols], ss_o.at[2 * d - 2 + cc], rs_o.at[2 * d - 2 + core],
                       ctx(y, x + d, cc))
            cp.start()
            sends.append(cp)
    for cc in range(2):
        cols = slice(768 * cc, 768 * cc + 768)

        @pl.when(core == cc)
        def _():
            wof[wo_rows, cols] = wo_ref[:, cols]

        @pl.when(core != cc)
        def _():
            rcopy(wo_ref.at[:, cols], wof.at[wo_rows, cols], ss_o.at[6], rs_o.at[6], sib).start()

    for j in range(6):
        wcat[128 * j + 96 : 128 * j + 128, :] = jnp.zeros((32, 1536), BF)
    for j in range(5):
        wcat[128 * j : 128 * j + 96, :] = convt_ref[96 * j : 96 * j + 96, :]
    r = lax.broadcasted_iota(jnp.int32, (96, 1536), 0) + 96 * me
    cc = lax.broadcasted_iota(jnp.int32, (96, 1536), 1)
    wcat[640:736, :] = jnp.where(r == cc, 1.0, 0.0).astype(BF)

    def comp(i, c):
        prod = lax.dot_general(embed_ref[...], wcat[pl.ds(_al(i * 256, 256), 256), :], (((1,), (1,)), ((), ())),
                               preferred_element_type=F32)
        wc[2 * i] = prod[:, 0:128]
        wc[2 * i + 1] = prod[:, 128:256]
        return c

    lax.fori_loop(0, 3, comp, 0)
    for b in range(4):
        for j in range(6):
            wcp[128 * b : 128 * b + 128, 128 * j : 128 * j + 128] = wc[j, pl.ds(b, 128, stride=4), :].astype(BF)
    yb[0:8, :] = jnp.zeros((8, 768), F32)
    yb[1288:1296, :] = jnp.zeros((8, 768), F32)

    def wait_b(d, c):
        bcopy(d).wait_recv()
        return c

    lax.fori_loop(1, 16, wait_b, 0)

    def taps(i, c):
        rows = pl.ds(_al(i * 256, 256), 256)
        bb = ball[rows, :].astype(F32)
        for b in range(4):
            oh[:, 128 * b : 128 * b + 128] = jnp.where(bb == float(b), 1.0, 0.0).astype(BF)
        yb[pl.ds(_al(i * 256 + 8, 8), 256), :] = _dot(oh[...], wcp[...])
        return c

    lax.fori_loop(0, 5, taps, 0)

    bias = convb_ref[...]

    def act(q, c):
        win = pl.ds(_al(q * 128, 8), 144)
        pre = jnp.zeros((128, 128), F32)
        for j in range(5):
            pre = pre + yb[win, 128 * j : 128 * j + 128][6 + j : 134 + j]
        own = yb[pl.ds(_al(q * 128 + 8, 8), 128), 640:768]
        val = own.T[0:96] + _gelu(pre.T[0:96] + bias)
        st[q // 5, :, pl.ds(_al(lax.rem(q, 5) * 128, 128), 128)] = val.astype(BF)
        return c

    own_rows = pl.ds(_al(me * 96, 16), 96)

    def s1(rel, ct):
        to = ctx(y, x + rel + 1, ct) if rel < 3 else ctx(1 - y, x, ct)
        return rcopy(st.at[ct], xt.at[own_rows], ss1.at[rel * 2 + ct], rs1.at[rel * 2 + core], to)

    for half in range(2):
        lax.fori_loop(5 * half, 5 * half + 5, act, 0)
        for rel in (3, 0, 2, 1):
            cp = s1(rel, half)
            cp.start()
            sends.append(cp)

        @pl.when(core == half)
        def _():
            xt[own_rows, :] = st[half]

        @pl.when(core != half)
        def _():
            rcopy(st.at[half], xt.at[own_rows], ss1.at[8], rs1.at[8], sib).start()

    def chip_rows(kk):
        return pl.ds(_al(kk * 192, 16), 192)

    def s1_wait(rel):
        for cs in range(2):
            rcopy(st.at[0], xt.at[own_rows], ss1.at[rel * 2 + cs], rs1.at[rel * 2 + cs], sib).wait_recv()

    s1_wait(3)
    ky = (1 - y) * 4 + x
    for d in (1, 3, 2):
        src = xt.at[chip_rows(ky), LA:640]
        cp = rcopy(src, src, ss2.at[2 + d], rs2.at[2 + d], ctx(y, x + d, core))
        cp.start()
        sends.append(cp)
    for d in (1, 3, 2):
        s1_wait(d - 1)
        src = xt.at[chip_rows(y * 4 + lax.rem(x + 4 - d, 4)), 0:LA]
        cp = rcopy(src, src, ss2.at[d - 1], rs2.at[d - 1], ctx(1 - y, x, core))
        cp.start()
        sends.append(cp)

    my_tok = pl.ds(_al(lax.rem(me, 8) * 80, 16), 80)
    cots = []
    for d in (1, 3, 2):
        for cc in range(2):
            cols = slice(768 * cc, 768 * cc + 768)
            cp = rcopy(cot_ref.at[:, cols], cotr.at[my_tok, cols], ss_c.at[2 * d - 2 + cc], rs_c.at[2 * d - 2 + core],
                       ctx(y, x + d, cc))
            cp.start()
            cots.append(cp)
    for cc in range(2):
        cols = slice(768 * cc, 768 * cc + 768)

        @pl.when(core == cc)
        def _():
            cotr[my_tok, cols] = cot_ref[:, cols]

        @pl.when(core != cc)
        def _():
            rcopy(cot_ref.at[:, cols], cotr.at[my_tok, cols], ss_c.at[6], rs_c.at[6], sib).start()

    def o_wait(slot):
        rcopy(wo_ref.at[:, 0:768], wof.at[0:64, 0:768], ss_o.at[0], rs_o.at[slot], sib).wait_recv()

    wo_cols = pl.ds(_al(core * 768, 128), 768)
    for slot in (0, 1, 4, 5, 2, 3, 6):
        o_wait(slot)
    for i, e in enumerate((1, 3)):
        part = wof.at[pl.ds(_al(y * 512 + 256 * i, 16), 256), wo_cols]
        cp = rcopy(part, part, ss_p.at[i], rs_p.at[i], ring_dev(e))
        cp.start()
        sends.append(cp)

    wcopy.wait()
    rcopy(st.at[0], xt.at[own_rows], ss1.at[8], rs1.at[8], sib).wait_recv()
    for d in (1, 3, 2):
        src = xt.at[chip_rows(0), LA:640]
        rcopy(src, src, ss2.at[2 + d], rs2.at[2 + d], sib).wait_recv()
        src = xt.at[chip_rows(0), 0:LA]
        rcopy(src, src, ss2.at[d - 1], rs2.at[d - 1], sib).wait_recv()

    def sq(i, acc):
        v = xt[pl.ds(_al(i * 128, 128), 128), :].astype(F32)
        return acc + jnp.sum((v * v).reshape(16, 8, 640), axis=0)

    total = lax.fori_loop(0, 12, sq, jnp.zeros((8, 640), F32))
    scale = lax.rsqrt(jnp.sum(total, axis=0, keepdims=True) * (1.0 / 1536.0) + 1e-06)
    for h in range(2):
        pr = _dot(wt[192 * h : 192 * h + 192, :], xt[...]) * scale
        qt[h] = (pr[0:64] * 0.125).astype(BF)
        kv[core, h] = pr[64:192].astype(BF)
    kcopy = rcopy(kv.at[core], kv.at[core], ss_k, rs_k, sib)
    kcopy.start()

    scopy = rcopy(sbuf.at[1 - core], sown, ss_s, rs_s, sib)

    @pl.when(core == y)
    def _():
        r = lax.broadcasted_iota(jnp.int32, (160, 640), 0) + 160 * x
        cidx = lax.broadcasted_iota(jnp.int32, (160, 640), 1)
        pick = jnp.where(r == cidx, 1.0, 0.0).astype(BF)
        for n in range(6):
            part = lax.dot_general(pick, xt[256 * n : 256 * n + 256, :], (((1,), (1,)), ((), ())),
                                   preferred_element_type=F32).astype(BF)
            sbuf[0, :, 256 * n : 256 * n + 256] = part[0:80]
            sbuf[1, :, 256 * n : 256 * n + 256] = part[80:160]
        sown[...] = sbuf[core]
        scopy.start()

    kcopy.wait()
    for h in range(2):
        for half in range(2):
            ks[h, 640 * half : 640 * half + 640, :] = kv[half, h, 0:64, :].astype(F32).T.astype(BF)

    steps = [(h, a, w) for a, w in ((0, 256), (256, 256), (512, 128)) for h in range(2)]

    def score(n):
        h, a, w = steps[n]
        sc[n % 2, :, 0:w] = _dot(ks[h], qt[h, :, a : a + w])

    score(0)
    outs = [None, None]
    for n, (h, a, w) in enumerate(steps):
        if n + 1 < len(steps):
            score(n + 1)
        s = sc[n % 2, :, 0:w]
        p = jnp.exp(s - jnp.max(s, axis=0, keepdims=True))
        den = jnp.sum(p, axis=0, keepdims=True)
        pb = p.astype(BF)
        o = (_dot(kv[0, h, 64:128, :], pb[0:640]) + _dot(kv[1, h, 64:128, :], pb[640:1280])) / den
        at[64 * h : 64 * h + 64, a : a + w] = o.astype(BF)
        outs[h] = o
        if h == 1:
            an[a : a + w, :] = jnp.concatenate(outs, axis=0).T.astype(BF)

    kx = core * 4 + x

    def tcopy(cc):
        return rcopy(at.at[64 * cc : 64 * cc + 64], ath.at[pl.ds(_al(y * 64, 16), 64)], ss_t.at[cc], rs_t.at[y],
                     kx * 2 + cc)

    for cc in range(2):
        @pl.when(kx * 2 + cc == me)
        def _():
            ath[pl.ds(_al(y * 64, 16), 64), :] = at[64 * cc : 64 * cc + 64, :]

        @pl.when(kx * 2 + cc != me)
        def _():
            tcopy(cc).start()

    def acopy(j):
        return rcopy(an.at[80 * j : 80 * j + 80], aown.at[:, pl.ds(_al(chip * 128, 128), 128)], ss_a.at[j], rs_a.at[chip],
                     8 * core + j)

    for j in range(8):
        @pl.when(8 * core + j == me)
        def _():
            aown[:, pl.ds(_al(chip * 128, 128), 128)] = an[80 * j : 80 * j + 80, :]

        @pl.when(8 * core + j != me)
        def _():
            acopy(j).start()

    for i in range(2):
        part = wof.at[0:256, wo_cols]
        rcopy(part, part, ss_p.at[i], rs_p.at[i], sib).wait_recv()
    ocopy = rcopy(wof.at[:, wo_cols], wof.at[:, wo_cols], ss_q, rs_q, sib)

    for d in (1, 3, 2):
        for cs in range(2):
            rcopy(cot_ref.at[:, 0:768], cotr.at[my_tok, 0:768], ss_c.at[2 * d - 2 + cs], rs_c.at[2 * d - 2 + cs],
                  sib).wait_recv()
    rcopy(cot_ref.at[:, 0:768], cotr.at[my_tok, 0:768], ss_c.at[6], rs_c.at[6], sib).wait_recv()
    half_cols = cotr.at[:, pl.ds(_al(core * 768, 128), 768)]
    dcopy = rcopy(half_cols, half_cols, ss_d, rs_d, sib)
    dcopy.start()
    ocopy.start()

    def t_wait(slot):
        rcopy(at.at[0:64], ath.at[0:64], ss_t.at[0], rs_t.at[slot], sib).wait_recv()

    t_wait(1 - y)

    @pl.when(core != y)
    def _():
        t_wait(y)

    dcopy.wait()
    for n in range(3):
        cols = slice(512 * n, 512 * n + 512)
        gl[:, cols] = _dot(ath[...], cotr[:, cols]).astype(BF)

    def block(r):
        return pl.ds(_al(lax.rem(r, 2) * 64, 16), 64), pl.ds(_al((r // 2) * 768, 128), 768)

    ysend = []
    for e in (1, 3, 2):
        rows, cols = block(lax.rem(ring + e, 4))
        cp = rcopy(gl.at[rows, cols], yr.at[e - 1], ss_y.at[e - 1], rs_y.at[e - 1], ring_dev(e))
        cp.start()
        ysend.append(cp)

    for k in range(8):
        @pl.when(2 * k + y != me)
        def _():
            rcopy(an.at[0:80], aown.at[:, 0:128], ss_a.at[0], rs_a.at[k], sib).wait_recv()

    @pl.when(core != y)
    def _():
        scopy.wait_recv()

    ocopy.wait()
    for n in range(6):
        cols = slice(256 * n, 256 * n + 256)
        out_ref[:, cols] = (sown[:, cols].astype(F32) + _dot(aown[...], wof[:, cols])).astype(BF)

    rows, cols = block(ring)
    acc = gl[rows, cols].astype(F32)
    for e, cp in zip((1, 3, 2), ysend):
        cp.wait_recv()
        acc = acc + yr[e - 1].astype(F32)
    zs[...] = acc.astype(BF)

    late = list(ysend)
    nsend = []
    for e in (1, 3, 2):
        cp = rcopy(zs.at[pl.ds(_al(lax.rem(zb + e, 4) * 16, 16), 16)], nr.at[e - 1], ss_n.at[e - 1], rs_n.at[e - 1], near(e))
        cp.start()
        nsend.append(cp)
    zrows = pl.ds(_al(zb * 16, 16), 16)
    acc = zs[zrows, :].astype(F32)
    for e, cp in zip((1, 3, 2), nsend):
        cp.wait_recv()
        acc = acc + nr[e - 1].astype(F32)
    fr[za] = acc.astype(BF)
    fsend = []
    for e in (2, 1, 3):
        cp = rcopy(fr.at[za], fr.at[za], ss_f.at[e - 1], rs_f.at[e - 1], far(e))
        cp.start()
        fsend.append(cp)
    for cp in fsend:
        cp.wait_recv()
    acc = fr[0].astype(F32)
    for s in range(1, 4):
        acc = acc + fr[s].astype(F32)
    rc[...] = acc.astype(BF)
    fcols = pl.ds(_al(yh * 768, 128), 768)
    fb[zrows, fcols] = rc[...]
    gsend = []
    for i, to in enumerate([across(e) for e in range(4)] + [near(e) for e in (1, 2, 3)]):
        cp = rcopy(rc, fb.at[zrows, fcols], ss_g.at[i], rs_g.at[i], to)
        cp.start()
        gsend.append(cp)
    for cp in gsend:
        cp.wait_recv()
    grad_ref[...] = fb[...]

    @pl.when(core == y)
    def _():
        scopy.wait_send()

    def send_b(d, c):
        bcopy(d).wait_send()
        return c

    lax.fori_loop(1, 16, send_b, 0)
    for cp in sends + cots + late + nsend + fsend + gsend:
        cp.wait_send()
    rcopy(st.at[0], xt.at[own_rows], ss1.at[8], rs1.at[8], sib).wait_send()
    rcopy(cot_ref.at[:, 0:768], cotr.at[my_tok, 0:768], ss_c.at[6], rs_c.at[6], sib).wait_send()
    rcopy(wo_ref.at[:, 0:768], wof.at[wo_rows, 0:768], ss_o.at[6], rs_o.at[6], sib).wait_send()
    for cc in range(2):
        @pl.when(kx * 2 + cc != me)
        def _():
            tcopy(cc).wait_send()
    for j in range(8):
        @pl.when(8 * core + j != me)
        def _():
            acopy(j).wait_send()


def per_device(bases, embed_w, conv_w, conv_b, norm_g, qkv_w, wo, cotangent):
    vm = pl.BlockSpec(memory_space=pltpu.VMEM)
    V = pltpu.VMEM

    def sems(n):
        return [pltpu.SemaphoreType.DMA((n,)), pltpu.SemaphoreType.DMA((n,))]

    one = [pltpu.SemaphoreType.DMA, pltpu.SemaphoreType.DMA]
    out, wo_grad = pl.pallas_call(
        layer_kernel,
        out_shape=(jax.ShapeDtypeStruct((80, 1536), BF), jax.ShapeDtypeStruct((64, 1536), BF)),
        in_specs=[vm] * 8,
        out_specs=(vm,) * 2,
        scratch_shapes=[
            V((80, 128), BF), V((1280, 128), BF), V((768, 1536), BF), V((6, 512, 128), F32), V((512, 768), BF),
            V((256, 512), BF), V((1296, 768), F32), V((2, 96, 640), BF), V((1536, 640), BF), V((384, 1536), BF),
            V((2, 64, 640), BF), V((2, 2, 128, 640), BF), V((2, 1280, 64), BF), V((2, 1280, 256), F32),
            V((128, 640), BF), V((640, 128), BF), V((128, 640), BF), V((80, 1024), BF), V((2, 80, 1536), BF),
            V((80, 1536), BF), V((640, 1536), BF), V((1024, 1536), BF),
            V((128, 1536), BF), V((3, 64, 768), BF), V((64, 768), BF), V((3, 16, 768), BF), V((4, 16, 768), BF),
            V((16, 768), BF), V((64, 1536), BF),
        ] + sems(15) + one + sems(9) + sems(6) + sems(7) + one + one + sems(2) + sems(8) + one + sems(7) + sems(2) + one
        + sems(3) + sems(3) + sems(3) + sems(7),
        compiler_params=pltpu.CompilerParams(collective_id=0, has_side_effects=True, vmem_limit_bytes=56 << 20),
        name="layer",
    )(bases.reshape(80, 128), embed_w, conv_w.transpose(0, 2, 1).reshape(480, 1536), conv_b.reshape(96, 1), qkv_w.T,
      norm_g[None], wo, cotangent[0])
    return out[None], wo_grad


def solution(mesh):
    return jax.shard_map(
        per_device,
        mesh=mesh,
        in_specs=(
            P("dp", "ctx"), P(), P(None, None, "ctx"), P("ctx"), P(), P(None, "ctx"), P("ctx", None),
            P("dp", "ctx", None),
        ),
        out_specs=(P("dp", "ctx", None), P("ctx", None)),
        check_vma=False,
    )
```

time: 136 us -> 94.2 us (0.69); the launches traced: 134 us -> 94 us
  Pallas kernels: 109 us -> 87.4 us
  between operations: 14.1 us -> 0.64 us
  matrix products: 3.3 us -> 0 us
    pallas_call x2 -> x1, Pallas kernels: 109 us -> 87.4 us  [per_device(): pl.pallas_call(layer_kernel, out_shape=(jax.ShapeDtypeStruct((80, 1536),...]
    dot_general x1 -> x0, matrix products: 3.3 us -> none  [_dot(): return jnp.dot(a, b, preferred_element_type=F32)]
    unnamed x10 -> x2, local copies, waits for them, and re-layouts: 5.45 us -> 3.27 us
    reshape x0 -> x1, local copies, waits for them, and re-layouts: none -> 1.37 us  [per_device(): conv_b.reshape(96, 1)]
  transfers between devices with their start and end apart: 1 -> 0, of which waited for: 0 -> 0; matrix products, arithmetic and copies ran while one was open for 4% -> 0% of each run, Pallas kernels for 81% -> 0%
where the time goes in v2:
time: 94.2 us; the launch traced here: 94 us
  Pallas kernels  87.4 us (93%)
  local copies, waits for them, and re-layouts  5.93 us (6%)
    pallas_call x1, Pallas kernels, per_device(): pl.pallas_call(layer_kernel, out_shape=(jax.ShapeDtypeStruct((80, 1536),...  87.4 us
    unnamed x2, local copies, waits for them, and re-layouts  3.27 us

profile of v2, /device:TPU:1, one launch (start us, length us, event | category | flops | bytes accessed | tf_op | source)
XLA Modules:
  0.0 94.0 jit_solution(15079263485055135284)
XLA Ops:
  0.6 1.3 %broadcast_in_dim.6.gain_ref = f32[1,1536]{1,0:T(1,128)} reshape(f32[1536]{0:T(1024)} %param.12) | data formatting | bytes 12288 | tf_op jit(solution)/shard_map/broadcast_in_dim | solution.py:471
  1.9 1.4 %copy.10.convb_ref = f32[96,1]{1,0:T(8,128)} copy(f32[96,1]{0,1:T(1,128)} %bitcast.13) | data formatting | bytes 768 | tf_op jit(solution)/shard_map/reshape | solution.py:470
  3.3 87.4 %layer.1 = (bf16[80,1536]{1,0:T(8,128)(2,1)}, bf16[64,1536]{1,0:T(8,128)(2,1)}) custom-call(s32[80,128]{1,0:T(8,128)} %bitcast.12, bf16[512,1536]{1,0:T(8,128)(2,1)} %embed_ref.1, bf16[480,1536]{1,0:T(8,128)(2,1)} %bitcast.8, f32[96,1]{1,0:T(8,128)} %copy.10.convb_ref, bf16[192,1536]{1,0:T(8,128)(2,1)} %bitcast.9, f32[1,1536]{1,0:T(1,128)} %broadcast_in_dim.6.gain_ref, ...), custom_call_target="tpu_custom_call" | custom-call | tf_op jit(solution)/shard_map/layer/pallas_call | solution.py:453
  90.7 1.7 %copy.13 = bf16[1,80,1536]{2,1,0:T(8,128)(2,1)} copy(bf16[1,80,1536]{2,1,0:T(8,128)(2,1)} %bitcast.11) | data formatting | bytes 491520
  92.3 1.6 %copy.14 = bf16[64,1536]{1,0:T(8,128)(2,1)} copy(bf16[64,1536]{1,0:T(8,128)(2,1)} %get-tuple-element.9) | data formatting | bytes 393216

commit v3 on v2

v3 whole, which is shorter than its diff:
```python
import functools

import jax
import jax.numpy as jnp
from jax import lax
from jax.experimental import pallas as pl
from jax.experimental.pallas import tpu as pltpu
from jax.sharding import PartitionSpec as P

MESH = pl.DeviceIdType.MESH
BF = jnp.bfloat16
F32 = jnp.float32
LA = 384


def _al(v, m):
    return pl.multiple_of(v, m)


def _dot(a, b):
    return jnp.dot(a, b, preferred_element_type=F32)


def _gelu(v):
    return 0.5 * v * (1.0 + jnp.tanh(0.7978845608028654 * (v + 0.044715 * (v * v * v))))


def layer_kernel(
    bases_hbm, embed_hbm, convt_hbm, convb_hbm, qkvt_hbm, gain_hbm, wo_hbm, cot_hbm,
    out_ref, grad_ref,
    ball, bsc, wcat, wc, wcp, oh, yb, st, xt, wt, qt, kv, ks, sc, at, an, ath, aown, sbuf, sown, cotr, wof,
    gl, yr, zs, nr, fr, rc, fb, acc, bases_ref, embed_ref, convb_ref, qkvt_ref, gain_ref, ld,
    ss_b, rs_b, ss_w, rs_w, ss1, rs1, ss2, rs2, ss_c, rs_c, ss_k, rs_k, ss_s, rs_s, ss_t, rs_t, ss_a, rs_a,
    ss_d, rs_d, ss_o, rs_o, ss_p, rs_p, ss_q, rs_q, ss_y, rs_y, ss_n, rs_n, ss_f, rs_f, ss_g, rs_g,
):
    dp = lax.axis_index("dp")
    me = lax.axis_index("ctx")
    yh, z = dp // 16, lax.rem(dp, 16)
    za, zb = z // 4, lax.rem(z, 4)
    core = lax.rem(me, 2)
    chip = me // 2
    x = lax.rem(chip, 4)
    y = me // 8
    sib = me + 1 - 2 * core
    ring = 2 * yh + y

    def ctx(yy, xx, cc):
        return (yy * 4 + lax.rem(xx, 4)) * 2 + cc

    def rcopy(src, dst, ssem, rsem, to):
        return pltpu.make_async_remote_copy(
            src_ref=src, dst_ref=dst, send_sem=ssem, recv_sem=rsem,
            device_id=to if isinstance(to, tuple) else (dp, to), device_id_type=MESH,
        )

    def ring_dev(e):
        r = lax.rem(ring + e, 4)
        return (r // 2) * 16 + z, lax.rem(r, 2) * 8 + lax.rem(me, 8)

    def near(e):
        return yh * 16 + za * 4 + lax.rem(zb + e, 4), me

    def across(e):
        return (1 - yh) * 16 + za * 4 + lax.rem(zb + e, 4), me

    def far(e):
        return yh * 16 + lax.rem(za + e, 4) * 4 + zb, me

    wo_rows = pl.ds(_al(me * 64, 16), 64)
    wo_other = pl.ds(_al((me + 8 - 16 * y) * 64, 16), 64)
    my_tok = pl.ds(_al(lax.rem(me, 8) * 80, 16), 80)
    barrier = pltpu.get_barrier_semaphore()
    greet = [(dp, lax.rem(me + d, 16)) for d in range(1, 16)]
    greet += [near(e) for e in (1, 2, 3)] + [far(e) for e in (1, 2, 3)] + [across(e) for e in range(4)]
    greet += [((1 - yh) * 16 + z, (1 - y) * 8 + lax.rem(me, 8))]
    for to in greet:
        pl.semaphore_signal(barrier, inc=1, device_id=to, device_id_type=MESH)
    loads = [
        pltpu.make_async_copy(src, dst, ld.at[i])
        for i, (src, dst) in enumerate(
            [(bases_hbm, bases_ref), (embed_hbm, embed_ref)]
            + [(convt_hbm.at[96 * j : 96 * j + 96], wcat.at[128 * j : 128 * j + 96]) for j in range(5)]
            + [(qkvt_hbm, qkvt_ref), (gain_hbm, gain_ref), (convb_hbm, convb_ref)]
            + [(wo_hbm, wof.at[wo_rows]), (cot_hbm, cotr.at[my_tok])]
        )
    ]
    for cp in loads:
        cp.start()
    loads[0].wait()
    ball[pl.ds(_al(me * 80, 16), 80), :] = bases_ref[...].astype(F32).astype(BF)
    pl.semaphore_wait(barrier, len(greet))

    plane = [(0, 1), (0, 3), (1, 0), (1, 1), (1, 3), (0, 2), (1, 2)]

    def ball_of(dev):
        return ball.at[pl.ds(_al(dev * 80, 16), 80)]

    def ysel(dy):
        return y + dy - 2 * dy * y

    bplane = []
    for i, (dy, dx) in enumerate(plane):
        cp = rcopy(ball_of(me), ball_of(me), ss_b.at[i], rs_b.at[i], ctx(ysel(dy), x + dx, core))
        cp.start()
        bplane.append(cp)
    bsib = [rcopy(ball_of(me), ball_of(me), ss_b.at[7], rs_b.at[7], sib)]
    bsib[0].start()

    for j in range(6):
        wcat[128 * j + 96 : 128 * j + 128, :] = jnp.zeros((32, 1536), BF)
    r = lax.broadcasted_iota(jnp.int32, (96, 1536), 0) + 96 * me
    cc = lax.broadcasted_iota(jnp.int32, (96, 1536), 1)
    wcat[640:736, :] = jnp.where(r == cc, 1.0, 0.0).astype(BF)
    for cp in loads[1:7]:
        cp.wait()

    def comp(i, c):
        prod = lax.dot_general(embed_ref[...], wcat[pl.ds(_al(i * 256, 256), 256), :], (((1,), (1,)), ((), ())),
                               preferred_element_type=F32)
        wc[2 * i] = prod[:, 0:128]
        wc[2 * i + 1] = prod[:, 128:256]
        return c

    lax.fori_loop(0, 2, comp, 0)
    for i, (dy, dx) in enumerate(plane):
        bplane[i].wait_recv()
        src = ball_of(ctx(ysel(dy), x + 4 - dx, core))
        cp = rcopy(src, src, ss_b.at[8 + i], rs_b.at[8 + i], sib)
        cp.start()
        bsib.append(cp)

    for cp in loads[7:12]:
        cp.wait()

    cots = []

    def send_cot(d):
        for cc in range(2):
            cols = slice(768 * cc, 768 * cc + 768)
            cp = rcopy(cotr.at[my_tok, cols], cotr.at[my_tok, cols], ss_c.at[2 * d - 2 + cc], rs_c.at[2 * d - 2 + core],
                       ctx(y, x + d, cc))
            cp.start()
            cots.append(cp)

    send_cot(1)
    send_cot(3)

    sends = []
    osib = []
    ocross = []
    for i, e in enumerate((1, 3)):
        cols = slice(768 * i, 768 * i + 768)
        cp = rcopy(wof.at[wo_rows, cols], wof.at[wo_rows, cols], ss_p.at[i], rs_p.at[i], ring_dev(e))
        cp.start()
        ocross.append(cp)
    wrows = pl.ds(_al(core * 192, 16), 192)
    for j in range(12):
        cols = slice(128 * j, 128 * j + 128)
        wt[wrows, cols] = (qkvt_ref[:, cols].astype(F32) * gain_ref[j : j + 1, :]).astype(BF)
    wcopy = rcopy(wt.at[wrows], wt.at[wrows], ss_w, rs_w, sib)
    wcopy.start()
    cp = rcopy(wof.at[wo_rows], wof.at[wo_rows], ss_q.at[0], rs_q.at[0], sib)
    cp.start()
    osib.append(cp)
    csib = [rcopy(cotr.at[my_tok], cotr.at[my_tok], ss_d.at[0], rs_d.at[0], sib)]
    csib[0].start()

    lax.fori_loop(2, 3, comp, 0)
    for b in range(4):
        for j in range(6):
            wcp[128 * b : 128 * b + 128, 128 * j : 128 * j + 128] = wc[j, pl.ds(b, 128, stride=4), :].astype(BF)
    yb[0:8, :] = jnp.zeros((8, 768), F32)
    yb[1288:1296, :] = jnp.zeros((8, 768), F32)
    bsc[...] = jnp.zeros((8, 128), F32)
    bsc[0:1, 0:96] = convb_ref[...]
    for cp in bsib:
        cp.wait_recv()

    def taps(i, c):
        rows = pl.ds(_al(i * 256, 256), 256)
        bb = ball[rows, :].astype(F32)
        for b in range(4):
            oh[:, 128 * b : 128 * b + 128] = jnp.where(bb == float(b), 1.0, 0.0).astype(BF)
        yb[pl.ds(_al(i * 256 + 8, 8), 256), :] = _dot(oh[...], wcp[...])
        return c


    bias = jnp.broadcast_to(bsc[0:1, :], (128, 128)).T[0:96]

    def act(q, c):
        win = pl.ds(_al(q * 128, 8), 144)
        pre = jnp.zeros((128, 128), F32)
        for j in range(5):
            pre = pre + yb[win, 128 * j : 128 * j + 128][6 + j : 134 + j]
        own = yb[pl.ds(_al(q * 128 + 8, 8), 128), 640:768]
        val = own.T[0:96] + _gelu(pre.T[0:96] + bias)
        st[q // 5, :, pl.ds(_al(lax.rem(q, 5) * 128, 128), 128)] = val.astype(BF)
        return c

    own_rows = pl.ds(_al(me * 96, 16), 96)

    def s1(rel, ct):
        to = ctx(y, x + rel + 1, ct) if rel < 3 else ctx(1 - y, x, ct)
        return rcopy(st.at[ct], xt.at[own_rows], ss1.at[rel * 2 + ct], rs1.at[rel * 2 + core], to)

    for half in range(2):
        lax.fori_loop(3 * half, 3 + 2 * half, taps, 0)
        lax.fori_loop(5 * half, 5 * half + 5, act, 0)
        for rel in (3, 0, 2, 1):
            cp = s1(rel, half)
            cp.start()
            sends.append(cp)

        @pl.when(core == half)
        def _():
            xt[own_rows, :] = st[half]

        @pl.when(core != half)
        def _():
            rcopy(st.at[half], xt.at[own_rows], ss1.at[8], rs1.at[8], sib).start()

    def chip_rows(kk):
        return pl.ds(_al(kk * 192, 16), 192)

    def s1_wait(rel):
        for cs in range(2):
            rcopy(st.at[0], xt.at[own_rows], ss1.at[rel * 2 + cs], rs1.at[rel * 2 + cs], sib).wait_recv()

    s1_wait(3)
    ky = (1 - y) * 4 + x
    for d in (1, 3, 2):
        src = xt.at[chip_rows(ky), LA:640]
        cp = rcopy(src, src, ss2.at[2 + d], rs2.at[2 + d], ctx(y, x + d, core))
        cp.start()
        sends.append(cp)
    for d in (1, 3, 2):
        s1_wait(d - 1)
        src = xt.at[chip_rows(y * 4 + lax.rem(x + 4 - d, 4)), 0:LA]
        cp = rcopy(src, src, ss2.at[d - 1], rs2.at[d - 1], ctx(1 - y, x, core))
        cp.start()
        sends.append(cp)

    send_cot(2)

    def cot_to_sib(d):
        for cs in range(2):
            rcopy(cotr.at[my_tok, 0:768], cotr.at[my_tok, 0:768], ss_c.at[0], rs_c.at[2 * d - 2 + cs], sib).wait_recv()
        part = cotr.at[pl.ds(_al(lax.rem(x + 4 - d, 4) * 160, 16), 160), pl.ds(_al(core * 768, 128), 768)]
        cp = rcopy(part, part, ss_d.at[d], rs_d.at[d], sib)
        cp.start()
        csib.append(cp)

    cot_to_sib(1)
    cot_to_sib(3)
    for cp in ocross:
        cp.wait_recv()
    cp = rcopy(wof.at[wo_other], wof.at[wo_other], ss_q.at[1], rs_q.at[1], sib)
    cp.start()
    osib.append(cp)
    ox = []
    for d in (1, 3, 2):
        for cc in range(2):
            for w, orows in enumerate((wo_rows, wo_other)):
                part = wof.at[orows, 768 * cc : 768 * cc + 768]
                i = (2 * d - 2) * 2 + w
                cp = rcopy(part, part, ss_o.at[i + 2 * cc], rs_o.at[i + 2 * core], ctx(y, x + d, cc))
                cp.start()
                ox.append(cp)

    wcopy.wait()
    rcopy(st.at[0], xt.at[own_rows], ss1.at[8], rs1.at[8], sib).wait_recv()

    def sq(i, tot):
        v = xt[pl.ds(_al(i * 128, 128), 128), :].astype(F32)
        return tot + jnp.sum((v * v).reshape(16, 8, 640), axis=0)

    def part(h, lo, hi, row):
        return _dot(wt[192 * h + lo : 192 * h + hi, pl.ds(_al(row * 768, 128), 768)], xt[pl.ds(_al(row * 768, 16), 768), :])

    total = lax.fori_loop(y * 6, y * 6 + 6, sq, jnp.zeros((8, 640), F32))
    for h in range(2):
        acc[h] = part(h, 0, 192, y)
    for d in (1, 3, 2):
        src = xt.at[chip_rows(0), LA:640]
        rcopy(src, src, ss2.at[2 + d], rs2.at[2 + d], sib).wait_recv()
        src = xt.at[chip_rows(0), 0:LA]
        rcopy(src, src, ss2.at[d - 1], rs2.at[d - 1], sib).wait_recv()
    total = lax.fori_loop(6 - y * 6, 12 - y * 6, sq, total)
    scale = lax.rsqrt(jnp.sum(total, axis=0, keepdims=True) * (1.0 / 1536.0) + 1e-06)
    kcopy = []
    for h in range(2):
        kv[core, h] = ((acc[h, 64:192] + part(h, 64, 192, 1 - y)) * scale).astype(BF)
        cp = rcopy(kv.at[core, h], kv.at[core, h], ss_k.at[h], rs_k.at[h], sib)
        cp.start()
        kcopy.append(cp)
    for h in range(2):
        qt[h] = ((acc[h, 0:64] + part(h, 0, 64, 1 - y)) * scale * 0.125).astype(BF)

    scopy = rcopy(sbuf.at[1 - core], sown, ss_s, rs_s, sib)

    @pl.when(core == y)
    def _():
        r = lax.broadcasted_iota(jnp.int32, (160, 640), 0) + 160 * x
        cidx = lax.broadcasted_iota(jnp.int32, (160, 640), 1)
        pick = jnp.where(r == cidx, 1.0, 0.0).astype(BF)
        for n in range(6):
            part = lax.dot_general(pick, xt[256 * n : 256 * n + 256, :], (((1,), (1,)), ((), ())),
                                   preferred_element_type=F32).astype(BF)
            sbuf[0, :, 256 * n : 256 * n + 256] = part[0:80]
            sbuf[1, :, 256 * n : 256 * n + 256] = part[80:160]
        sown[...] = sbuf[core]
        scopy.start()

    for cp in kcopy:
        cp.wait()
    for h in range(2):
        for half in range(2):
            ks[h, 640 * half : 640 * half + 640, :] = kv[half, h, 0:64, :].astype(F32).T.astype(BF)

    steps = [(h, a, w) for a, w in ((0, 256), (256, 256), (512, 128)) for h in range(2)]

    def score(n):
        h, a, w = steps[n]
        sc[n % 2, :, 0:w] = _dot(ks[h], qt[h, :, a : a + w])

    kx = core * 4 + x
    trows = pl.ds(_al(y * 64, 16), 64)
    tiles = ((0, 256), (256, 256), (512, 128))

    def tcopy(t, cc):
        a, w = tiles[t]
        return rcopy(at.at[64 * cc : 64 * cc + 64, a : a + w], ath.at[trows, a : a + w], ss_t.at[2 * t + cc],
                     rs_t.at[2 * t + y], kx * 2 + cc)

    def acopy(j):
        return rcopy(an.at[80 * j : 80 * j + 80], aown.at[:, pl.ds(_al(chip * 128, 128), 128)], ss_a.at[j], rs_a.at[chip],
                     8 * core + j)

    score(0)
    outs = [None, None]
    for n, (h, a, w) in enumerate(steps):
        if n + 1 < len(steps):
            score(n + 1)
        s = sc[n % 2, :, 0:w]
        p = jnp.exp(s - jnp.max(s, axis=0, keepdims=True))
        den = jnp.sum(p, axis=0, keepdims=True)
        pb = p.astype(BF)
        o = (_dot(kv[0, h, 64:128, :], pb[0:640]) + _dot(kv[1, h, 64:128, :], pb[640:1280])) / den
        at[64 * h : 64 * h + 64, a : a + w] = o.astype(BF)
        outs[h] = o
        if h == 1:
            t = n // 2
            for cc in range(2):
                @pl.when(kx * 2 + cc == me)
                def _():
                    ath[trows, a : a + w] = at[64 * cc : 64 * cc + 64, a : a + w]

                @pl.when(kx * 2 + cc != me)
                def _():
                    tcopy(t, cc).start()
            an[a : a + w, :] = jnp.concatenate(outs, axis=0).T.astype(BF)
            for j in ((0, 1, 2), (3, 4, 5), (6, 7))[t]:
                @pl.when(8 * core + j == me)
                def _():
                    aown[:, pl.ds(_al(chip * 128, 128), 128)] = an[80 * j : 80 * j + 80, :]

                @pl.when(8 * core + j != me)
                def _():
                    acopy(j).start()

    cot_to_sib(2)

    def t_wait(yy):
        for t in range(3):
            a, w = tiles[t]
            rcopy(at.at[0:64, a : a + w], ath.at[0:64, a : a + w], ss_t.at[0], rs_t.at[2 * t + yy], sib).wait_recv()

    t_wait(1 - y)

    @pl.when(core != y)
    def _():
        t_wait(y)

    for cp in csib:
        cp.wait_recv()

    def block(r, i):
        return pl.ds(_al(lax.rem(r, 2) * 64, 16), 64), pl.ds(_al((r // 2) * 768 + 384 * i, 128), 384)

    ysend, nsend, fsend, gsend = [[], []], [[], []], [[], []], [[], []]
    for i in range(2):
        for hh in range(2):
            cols = slice(768 * hh + 384 * i, 768 * hh + 384 * i + 384)
            gl[:, cols] = _dot(ath[...], cotr[:, cols]).astype(BF)
        for e in (1, 3, 2):
            rows, cols = block(lax.rem(ring + e, 4), i)
            k = 3 * i + e - 1
            cp = rcopy(gl.at[rows, cols], yr.at[k], ss_y.at[k], rs_y.at[k], ring_dev(e))
            cp.start()
            ysend[i].append(cp)

    for i in range(2):
        rows, cols = block(ring, i)
        acc = gl[rows, cols].astype(F32)
        for e, cp in zip((1, 3, 2), ysend[i]):
            cp.wait_recv()
            acc = acc + yr[3 * i + e - 1].astype(F32)
        zs[i] = acc.astype(BF)
        for e in (1, 3, 2):
            k = 3 * i + e - 1
            cp = rcopy(zs.at[i, pl.ds(_al(lax.rem(zb + e, 4) * 16, 16), 16)], nr.at[k], ss_n.at[k], rs_n.at[k], near(e))
            cp.start()
            nsend[i].append(cp)
    zrows = pl.ds(_al(zb * 16, 16), 16)
    for i in range(2):
        acc = zs[i, zrows, :].astype(F32)
        for e, cp in zip((1, 3, 2), nsend[i]):
            cp.wait_recv()
            acc = acc + nr[3 * i + e - 1].astype(F32)
        fr[i, za] = acc.astype(BF)
        for e in (2, 1, 3):
            k = 3 * i + e - 1
            cp = rcopy(fr.at[i, za], fr.at[i, za], ss_f.at[k], rs_f.at[k], far(e))
            cp.start()
            fsend[i].append(cp)
    for i in range(2):
        for cp in fsend[i]:
            cp.wait_recv()
        acc = fr[i, 0].astype(F32)
        for q in range(1, 4):
            acc = acc + fr[i, q].astype(F32)
        rc[i] = acc.astype(BF)
        fcols = pl.ds(_al(yh * 768 + 384 * i, 128), 384)
        fb[zrows, fcols] = rc[i]
        for k, to in enumerate([across(e) for e in range(4)] + [near(e) for e in (1, 2, 3)]):
            cp = rcopy(rc.at[i], fb.at[zrows, fcols], ss_g.at[7 * i + k], rs_g.at[7 * i + k], to)
            cp.start()
            gsend[i].append(cp)

    wo_cols = pl.ds(_al(core * 768, 128), 768)
    for d in (1, 3, 2):
        for i in range(4):
            rcopy(wof.at[0:64, 0:768], wof.at[0:64, 0:768], ss_o.at[0], rs_o.at[(2 * d - 2) * 2 + i], sib).wait_recv()
        for yy in range(2):
            part = wof.at[pl.ds(_al((yy * 4 + lax.rem(x + 4 - d, 4)) * 128, 16), 128), wo_cols]
            k = 2 + (d - 1) * 2 + yy
            cp = rcopy(part, part, ss_q.at[k], rs_q.at[k], sib)
            cp.start()
            osib.append(cp)
    for k in range(8):
        @pl.when(2 * k + y != me)
        def _():
            rcopy(an.at[0:80], aown.at[:, 0:128], ss_a.at[0], rs_a.at[k], sib).wait_recv()

    @pl.when(core != y)
    def _():
        scopy.wait_recv()

    for cp in osib:
        cp.wait_recv()
    for n in range(6):
        cols = slice(256 * n, 256 * n + 256)
        out_ref[:, cols] = (sown[:, cols].astype(F32) + _dot(aown[...], wof[:, cols])).astype(BF)

    for i in range(2):
        for cp in gsend[i]:
            cp.wait_recv()
    grad_ref[...] = fb[...]

    @pl.when(core == y)
    def _():
        scopy.wait_send()

    for cp in sends + bplane + bsib + ocross + osib + ox + cots + csib:
        cp.wait_send()
    for i in range(2):
        for cp in ysend[i] + nsend[i] + fsend[i] + gsend[i]:
            cp.wait_send()
    rcopy(st.at[0], xt.at[own_rows], ss1.at[8], rs1.at[8], sib).wait_send()
    for cc in range(2):
        @pl.when(kx * 2 + cc != me)
        def _():
            for t in range(3):
                tcopy(t, cc).wait_send()
    for j in range(8):
        @pl.when(8 * core + j != me)
        def _():
            acopy(j).wait_send()


def place_kernel(a_ref, b_ref, oa_ref, ob_ref):
    oa_ref[...] = a_ref[...]
    ob_ref[...] = b_ref[...]


def per_device(bases, embed_w, conv_w, conv_b, norm_g, qkv_w, wo, cotangent):
    vm = pl.BlockSpec(memory_space=pltpu.VMEM)
    V = pltpu.VMEM

    def sems(n):
        return [pltpu.SemaphoreType.DMA((n,)), pltpu.SemaphoreType.DMA((n,))]

    one = [pltpu.SemaphoreType.DMA, pltpu.SemaphoreType.DMA]
    out, wo_grad = pl.pallas_call(
        layer_kernel,
        out_shape=(jax.ShapeDtypeStruct((80, 1536), BF), jax.ShapeDtypeStruct((64, 1536), BF)),
        in_specs=[pl.BlockSpec(memory_space=pltpu.HBM)] * 8,
        out_specs=(vm,) * 2,
        scratch_shapes=[
            V((1280, 128), BF), V((8, 128), F32), V((768, 1536), BF), V((6, 512, 128), F32), V((512, 768), BF),
            V((256, 512), BF), V((1296, 768), F32), V((2, 96, 640), BF), V((1536, 640), BF), V((384, 1536), BF),
            V((2, 64, 640), BF), V((2, 2, 128, 640), BF), V((2, 1280, 64), BF), V((2, 1280, 256), F32),
            V((128, 640), BF), V((640, 128), BF), V((128, 640), BF), V((80, 1024), BF), V((2, 80, 1536), BF),
            V((80, 1536), BF), V((640, 1536), BF), V((1024, 1536), BF),
            V((128, 1536), BF), V((6, 64, 384), BF), V((2, 64, 384), BF), V((6, 16, 384), BF), V((2, 4, 16, 384), BF),
            V((2, 16, 384), BF), V((64, 1536), BF), V((2, 192, 640), F32),
            V((80, 128), jnp.int32), V((512, 1536), BF), V((1, 96), F32), V((192, 1536), BF), V((12, 128), F32),
            pltpu.SemaphoreType.DMA((12,)),
        ] + sems(15) + one + sems(9) + sems(6) + sems(6) + sems(2) + one + sems(6) + sems(8) + sems(4) + sems(12) + sems(2)
        + sems(8) + sems(6) + sems(6) + sems(6) + sems(14),
        compiler_params=pltpu.CompilerParams(collective_id=0, has_side_effects=True, vmem_limit_bytes=56 << 20),
        name="layer",
    )(bases.reshape(80, 128), embed_w, conv_w.transpose(0, 2, 1).reshape(480, 1536), conv_b[None], qkv_w.T,
      norm_g.reshape(12, 128), wo, cotangent[0])
    out, wo_grad = pl.pallas_call(
        place_kernel,
        out_shape=(jax.ShapeDtypeStruct((80, 1536), BF), jax.ShapeDtypeStruct((64, 1536), BF)),
        in_specs=[vm] * 2,
        out_specs=(vm,) * 2,
        name="place",
    )(out, wo_grad)
    return out[None], wo_grad


def solution(mesh):
    return jax.shard_map(
        per_device,
        mesh=mesh,
        in_specs=(
            P("dp", "ctx"), P(), P(None, None, "ctx"), P("ctx"), P(), P(None, "ctx"), P("ctx", None),
            P("dp", "ctx", None),
        ),
        out_specs=(P("dp", "ctx", None), P("ctx", None)),
        check_vma=False,
    )
```

time: 94.2 us -> 83.5 us (0.89)
  local copies, waits for them, and re-layouts: 5.93 us -> 0 us
  Pallas kernels: 87.4 us -> 82.7 us
    pallas_call x1, Pallas kernels: 87.4 us -> 80.8 us  [per_device(): pl.pallas_call(layer_kernel, out_shape=(jax.ShapeDtypeStruct((80, 1536),...]
    unnamed x2 -> x0, local copies, waits for them, and re-layouts: 3.27 us -> none
    pallas_call x0 -> x1, Pallas kernels: none -> 1.82 us  [per_device(): pl.pallas_call(place_kernel, out_shape=(jax.ShapeDtypeStruct((80, 1536),...]
    reshape x1 -> x0, local copies, waits for them, and re-layouts: 1.37 us -> none  [per_device(): conv_b.reshape(96, 1)]
    broadcast_in_dim x1 -> x0, local copies, waits for them, and re-layouts: 1.29 us -> none  [per_device(): norm_g[None]]
where the time goes in v3:
time: 83.5 us; the launch traced here: 83.3 us
  Pallas kernels  82.7 us (99%)
    pallas_call x1, Pallas kernels, per_device(): pl.pallas_call(layer_kernel, out_shape=(jax.ShapeDtypeStruct((80, 1536),...  80.8 us
    pallas_call x1, Pallas kernels, per_device(): pl.pallas_call(place_kernel, out_shape=(jax.ShapeDtypeStruct((80, 1536),...  1.82 us

profile of v3, /device:TPU:1, one launch (start us, length us, event | category | flops | bytes accessed | tf_op | source)
XLA Modules:
  0.0 83.3 jit_solution(6286487842254397947)
XLA Ops:
  0.6 80.8 %layer.1 = (bf16[80,1536]{1,0:T(8,128)(2,1)}, bf16[64,1536]{1,0:T(8,128)(2,1)}) custom-call(s32[80,128]{1,0:T(8,128)} %bitcast.12, bf16[512,1536]{1,0:T(8,128)(2,1)} %embed_hbm.1, bf16[480,1536]{1,0:T(8,128)(2,1)} %bitcast.9, f32[1,96]{1,0:T(1,128)} %bitcast.14, bf16[192,1536]{1,0:T(8,128)(2,1)} %bitcast.10, f32[12,128]{1,0:T(8,128)} %bitcast.13, ...), custom_call_target="tpu_custom_call" | custom-call | tf_op jit(solution)/shard_map/layer/pallas_call | solution.py:504
  81.5 1.8 %place.1 = (bf16[80,1536]{1,0:T(8,128)(2,1)}, bf16[64,1536]{1,0:T(8,128)(2,1)}) custom-call(bf16[80,1536]{1,0:T(8,128)(2,1)} %get-tuple-element.6.a_ref, bf16[64,1536]{1,0:T(8,128)(2,1)} %get-tuple-element.7.b_ref), custom_call_target="tpu_custom_call" | custom-call | tf_op jit(solution)/shard_map/place/pallas_call | solution.py:525

commit v4 on v3

--- a/solution.py
+++ b/solution.py
@@ -10,7 +10,7 @@
 MESH = pl.DeviceIdType.MESH
 BF = jnp.bfloat16
 F32 = jnp.float32
-LA = 384
+LA = 256
 
 
 def _al(v, m):
@@ -29,9 +29,10 @@
     bases_hbm, embed_hbm, convt_hbm, convb_hbm, qkvt_hbm, gain_hbm, wo_hbm, cot_hbm,
     out_ref, grad_ref,
     ball, bsc, wcat, wc, wcp, oh, yb, st, xt, wt, qt, kv, ks, sc, at, an, ath, aown, sbuf, sown, cotr, wof,
+    pbuf, prx, pown, obuf, orx,
     gl, yr, zs, nr, fr, rc, fb, acc, bases_ref, embed_ref, convb_ref, qkvt_ref, gain_ref, ld,
     ss_b, rs_b, ss_w, rs_w, ss1, rs1, ss2, rs2, ss_c, rs_c, ss_k, rs_k, ss_s, rs_s, ss_t, rs_t, ss_a, rs_a,
-    ss_d, rs_d, ss_o, rs_o, ss_p, rs_p, ss_q, rs_q, ss_y, rs_y, ss_n, rs_n, ss_f, rs_f, ss_g, rs_g,
+    ss_d, rs_d, ss_o, rs_o, ss_p, rs_p, ss_q, rs_q, ss3, rs3, ss4, rs4, ss_y, rs_y, ss_n, rs_n, ss_f, rs_f, ss_g, rs_g,
 ):
     dp = lax.axis_index("dp")
     me = lax.axis_index("ctx")
@@ -66,8 +67,7 @@
     def far(e):
         return yh * 16 + lax.rem(za + e, 4) * 4 + zb, me
 
-    wo_rows = pl.ds(_al(me * 64, 16), 64)
-    wo_other = pl.ds(_al((me + 8 - 16 * y) * 64, 16), 64)
+    wo_rows = pl.ds(_al(lax.rem(me, 8) * 64, 16), 64)
     my_tok = pl.ds(_al(lax.rem(me, 8) * 80, 16), 80)
     barrier = pltpu.get_barrier_semaphore()
     greet = [(dp, lax.rem(me + d, 16)) for d in range(1, 16)]
@@ -146,22 +146,19 @@
     send_cot(3)
 
     sends = []
-    osib = []
-    ocross = []
-    for i, e in enumerate((1, 3)):
-        cols = slice(768 * i, 768 * i + 768)
-        cp = rcopy(wof.at[wo_rows, cols], wof.at[wo_rows, cols], ss_p.at[i], rs_p.at[i], ring_dev(e))
-        cp.start()
-        ocross.append(cp)
     wrows = pl.ds(_al(core * 192, 16), 192)
     for j in range(12):
         cols = slice(128 * j, 128 * j + 128)
         wt[wrows, cols] = (qkvt_ref[:, cols].astype(F32) * gain_ref[j : j + 1, :]).astype(BF)
     wcopy = rcopy(wt.at[wrows], wt.at[wrows], ss_w, rs_w, sib)
     wcopy.start()
-    cp = rcopy(wof.at[wo_rows], wof.at[wo_rows], ss_q.at[0], rs_q.at[0], sib)
-    cp.start()
-    osib.append(cp)
+    for cc in range(2):
+        cols = slice(768 * cc, 768 * cc + 768)
+
+        @pl.when(core != cc)
+        def _():
+            rcopy(wof.at[wo_rows, cols], wof.at[wo_rows, cols], ss_o.at[6], rs_o.at[6], sib).start()
+
     csib = [rcopy(cotr.at[my_tok], cotr.at[my_tok], ss_d.at[0], rs_d.at[0], sib)]
     csib[0].start()
 
@@ -206,7 +203,7 @@
     for half in range(2):
         lax.fori_loop(3 * half, 3 + 2 * half, taps, 0)
         lax.fori_loop(5 * half, 5 * half + 5, act, 0)
-        for rel in (3, 0, 2, 1):
+        for rel in (3, 0, 2):
             cp = s1(rel, half)
             cp.start()
             sends.append(cp)
@@ -226,46 +223,60 @@
         for cs in range(2):
             rcopy(st.at[0], xt.at[own_rows], ss1.at[rel * 2 + cs], rs1.at[rel * 2 + cs], sib).wait_recv()
 
+    def chip_at(yy, d):
+        return yy * 4 + lax.rem(x + d, 4)
+
+    def push(ref, ssem, rsem, to):
+        cp = rcopy(ref, ref, ssem, rsem, to)
+        cp.start()
+        sends.append(cp)
+
+    def to_y(d):
+        push(xt.at[chip_rows(chip_at(y, 4 - d)), 0:LA], ss2.at[d - 1], rs2.at[d - 1], ctx(1 - y, x, core))
+
+    def half_rows(kk, i):
+        return pl.ds(_al(kk * 192 + 96 * i, 16), 96)
+
     s1_wait(3)
-    ky = (1 - y) * 4 + x
-    for d in (1, 3, 2):
-        src = xt.at[chip_rows(ky), LA:640]
-        cp = rcopy(src, src, ss2.at[2 + d], rs2.at[2 + d], ctx(y, x + d, core))
-        cp.start()
-        sends.append(cp)
-    for d in (1, 3, 2):
+    for d in (1, 3):
+        push(xt.at[chip_rows(chip_at(1 - y, 0)), LA:640], ss2.at[2 + d], rs2.at[2 + d], ctx(y, x + d, core))
+    for i, d in ((0, 1), (1, 3)):
         s1_wait(d - 1)
-        src = xt.at[chip_rows(y * 4 + lax.rem(x + 4 - d, 4)), 0:LA]
-        cp = rcopy(src, src, ss2.at[d - 1], rs2.at[d - 1], ctx(1 - y, x, core))
-        cp.start()
-        sends.append(cp)
-
-    send_cot(2)
+        to_y(d)
+        push(xt.at[half_rows(chip_at(y, 4 - d), i)], ss3.at[i], rs3.at[i], ctx(y, x + d, core))
+    for i in range(2):
+        rcopy(st.at[0], xt.at[own_rows], ss3.at[i], rs3.at[i], sib).wait_recv()
+    to_y(2)
+    for i, d in ((0, 1), (1, 3)):
+        src = xt.at[chip_rows(0), LA:640]
+        rcopy(src, src, ss2.at[2 + d], rs2.at[2 + d], sib).wait_recv()
+        push(xt.at[half_rows(chip_at(1 - y, 4 - d), i), LA:640], ss4.at[i], rs4.at[i], ctx(y, x + d, core))
+
+    core_cols = pl.ds(_al(core * 768, 128), 768)
+
+    def cot_rows(d, i, n):
+        return pl.ds(_al(lax.rem(x + 4 - d, 4) * 160 + 80 * i, 16), n)
 
     def cot_to_sib(d):
+        part = cotr.at[cot_rows(d, 0, 160), core_cols]
+        cp = rcopy(part, part, ss_d.at[d], rs_d.at[d], sib)
+        cp.start()
+        csib.append(cp)
+
+    for i, d in ((0, 1), (1, 3)):
         for cs in range(2):
             rcopy(cotr.at[my_tok, 0:768], cotr.at[my_tok, 0:768], ss_c.at[0], rs_c.at[2 * d - 2 + cs], sib).wait_recv()
-        part = cotr.at[pl.ds(_al(lax.rem(x + 4 - d, 4) * 160, 16), 160), pl.ds(_al(core * 768, 128), 768)]
-        cp = rcopy(part, part, ss_d.at[d], rs_d.at[d], sib)
-        cp.start()
-        csib.append(cp)
-
-    cot_to_sib(1)
-    cot_to_sib(3)
-    for cp in ocross:
-        cp.wait_recv()
-    cp = rcopy(wof.at[wo_other], wof.at[wo_other], ss_q.at[1], rs_q.at[1], sib)
-    cp.start()
-    osib.append(cp)
-    ox = []
+        part = cotr.at[cot_rows(d, i, 80), core_cols]
+        cp = rcopy(part, part, ss_c.at[2 + i], rs_c.at[2 + i], ctx(y, x + d, core))
+        cp.start()
+        cots.append(cp)
+        cot_to_sib(d)
     for d in (1, 3, 2):
         for cc in range(2):
-            for w, orows in enumerate((wo_rows, wo_other)):
-                part = wof.at[orows, 768 * cc : 768 * cc + 768]
-                i = (2 * d - 2) * 2 + w
-                cp = rcopy(part, part, ss_o.at[i + 2 * cc], rs_o.at[i + 2 * core], ctx(y, x + d, cc))
-                cp.start()
-                ox.append(cp)
+            part = wof.at[wo_rows, 768 * cc : 768 * cc + 768]
+            cp = rcopy(part, part, ss_o.at[2 * d - 2 + cc], rs_o.at[2 * d - 2 + core], ctx(y, x + d, cc))
+            cp.start()
+            sends.append(cp)
 
     wcopy.wait()
     rcopy(st.at[0], xt.at[own_rows], ss1.at[8], rs1.at[8], sib).wait_recv()
@@ -281,10 +292,11 @@
     for h in range(2):
         acc[h] = part(h, 0, 192, y)
     for d in (1, 3, 2):
-        src = xt.at[chip_rows(0), LA:640]
-        rcopy(src, src, ss2.at[2 + d], rs2.at[2 + d], sib).wait_recv()
         src = xt.at[chip_rows(0), 0:LA]
         rcopy(src, src, ss2.at[d - 1], rs2.at[d - 1], sib).wait_recv()
+    for i in range(2):
+        src = xt.at[own_rows, LA:640]
+        rcopy(src, src, ss4.at[i], rs4.at[i], sib).wait_recv()
     total = lax.fori_loop(6 - y * 6, 12 - y * 6, sq, total)
     scale = lax.rsqrt(jnp.sum(total, axis=0, keepdims=True) * (1.0 / 1536.0) + 1e-06)
     kcopy = []
@@ -304,10 +316,8 @@
         cidx = lax.broadcasted_iota(jnp.int32, (160, 640), 1)
         pick = jnp.where(r == cidx, 1.0, 0.0).astype(BF)
         for n in range(6):
-            part = lax.dot_general(pick, xt[256 * n : 256 * n + 256, :], (((1,), (1,)), ((), ())),
-                                   preferred_element_type=F32).astype(BF)
-            sbuf[0, :, 256 * n : 256 * n + 256] = part[0:80]
-            sbuf[1, :, 256 * n : 256 * n + 256] = part[80:160]
+            sbuf[n // 3, :, 256 * (n % 3) : 256 * (n % 3) + 256] = lax.dot_general(
+                pick, xt[256 * n : 256 * n + 256, :], (((1,), (1,)), ((), ())), preferred_element_type=F32).astype(BF)
         sown[...] = sbuf[core]
         scopy.start()
 
@@ -332,9 +342,12 @@
         return rcopy(at.at[64 * cc : 64 * cc + 64, a : a + w], ath.at[trows, a : a + w], ss_t.at[2 * t + cc],
                      rs_t.at[2 * t + y], kx * 2 + cc)
 
-    def acopy(j):
-        return rcopy(an.at[80 * j : 80 * j + 80], aown.at[:, pl.ds(_al(chip * 128, 128), 128)], ss_a.at[j], rs_a.at[chip],
-                     8 * core + j)
+    def acopy(d, cc):
+        return rcopy(an.at[pl.ds(_al(lax.rem(x + d, 4) * 160, 16), 160)], aown.at[a_rows, a_cols], ss_a.at[2 * d + cc],
+                     rs_a.at[2 * d + core], ctx(y, x + d, cc))
+
+    a_rows = pl.ds(_al(core * 160, 16), 160)
+    a_cols = pl.ds(_al(x * 128, 128), 128)
 
     score(0)
     outs = [None, None]
@@ -359,15 +372,18 @@
                 def _():
                     tcopy(t, cc).start()
             an[a : a + w, :] = jnp.concatenate(outs, axis=0).T.astype(BF)
-            for j in ((0, 1, 2), (3, 4, 5), (6, 7))[t]:
-                @pl.when(8 * core + j == me)
-                def _():
-                    aown[:, pl.ds(_al(chip * 128, 128), 128)] = an[80 * j : 80 * j + 80, :]
-
-                @pl.when(8 * core + j != me)
-                def _():
-                    acopy(j).start()
-
+
+    aown[a_rows, a_cols] = an[pl.ds(_al(x * 160, 16), 160), :]
+    for d in (1, 3, 2):
+        for cc in range(2):
+            acopy(d, cc).start()
+    for cc in range(2):
+        @pl.when(core != cc)
+        def _():
+            acopy(0, cc).start()
+
+    for i in range(2):
+        rcopy(cotr.at[my_tok, 0:768], cotr.at[my_tok, 0:768], ss_c.at[0], rs_c.at[2 + i], sib).wait_recv()
     cot_to_sib(2)
 
     def t_wait(yy):
@@ -423,6 +439,16 @@
             cp = rcopy(fr.at[i, za], fr.at[i, za], ss_f.at[k], rs_f.at[k], far(e))
             cp.start()
             fsend[i].append(cp)
+    for i in range(7):
+        rcopy(wof.at[0:64, 0:768], wof.at[0:64, 0:768], ss_o.at[0], rs_o.at[i], sib).wait_recv()
+    for i in range(2, 8):
+        rcopy(an.at[0:160], aown.at[0:160, 0:128], ss_a.at[0], rs_a.at[i], sib).wait_recv()
+    rcopy(an.at[0:160], aown.at[0:160, 0:128], ss_a.at[0], rs_a.at[1 - core], sib).wait_recv()
+    pbuf[...] = _dot(aown[pl.ds(_al((1 - y) * 160, 16), 160), :], wof[:, core_cols]).astype(BF)
+    pcopy = rcopy(pbuf, prx, ss_p, rs_p, ctx(1 - y, x, core))
+    pcopy.start()
+    pown[...] = _dot(aown[pl.ds(_al(y * 160, 16), 160), :], wof[:, core_cols])
+
     for i in range(2):
         for cp in fsend[i]:
             cp.wait_recv()
@@ -437,41 +463,30 @@
             cp.start()
             gsend[i].append(cp)
 
-    wo_cols = pl.ds(_al(core * 768, 128), 768)
-    for d in (1, 3, 2):
-        for i in range(4):
-            rcopy(wof.at[0:64, 0:768], wof.at[0:64, 0:768], ss_o.at[0], rs_o.at[(2 * d - 2) * 2 + i], sib).wait_recv()
-        for yy in range(2):
-            part = wof.at[pl.ds(_al((yy * 4 + lax.rem(x + 4 - d, 4)) * 128, 16), 128), wo_cols]
-            k = 2 + (d - 1) * 2 + yy
-            cp = rcopy(part, part, ss_q.at[k], rs_q.at[k], sib)
-            cp.start()
-            osib.append(cp)
-    for k in range(8):
-        @pl.when(2 * k + y != me)
-        def _():
-            rcopy(an.at[0:80], aown.at[:, 0:128], ss_a.at[0], rs_a.at[k], sib).wait_recv()
-
     @pl.when(core != y)
     def _():
         scopy.wait_recv()
 
-    for cp in osib:
-        cp.wait_recv()
-    for n in range(6):
-        cols = slice(256 * n, 256 * n + 256)
-        out_ref[:, cols] = (sown[:, cols].astype(F32) + _dot(aown[...], wof[:, cols])).astype(BF)
+    pcopy.wait_recv()
+    whole = (sown[...].astype(F32) + (pown[...] + prx[...].astype(F32))).astype(BF)
+    obuf[0] = whole[0:80]
+    obuf[1] = whole[80:160]
+    ocopy = rcopy(obuf.at[1 - core], orx, ss_q, rs_q, sib)
+    ocopy.start()
+    out_ref[:, core_cols] = obuf[core]
 
     for i in range(2):
         for cp in gsend[i]:
             cp.wait_recv()
     grad_ref[...] = fb[...]
+    ocopy.wait_recv()
+    out_ref[:, pl.ds(_al(768 - core * 768, 128), 768)] = orx[...]
 
     @pl.when(core == y)
     def _():
         scopy.wait_send()
 
-    for cp in sends + bplane + bsib + ocross + osib + ox + cots + csib:
+    for cp in sends + bplane + bsib + cots + csib + [pcopy, ocopy]:
         cp.wait_send()
     for i in range(2):
         for cp in ysend[i] + nsend[i] + fsend[i] + gsend[i]:
@@ -482,10 +497,14 @@
         def _():
             for t in range(3):
                 tcopy(t, cc).wait_send()
-    for j in range(8):
-        @pl.when(8 * core + j != me)
+    for d in (1, 3, 2):
+        for cc in range(2):
+            acopy(d, cc).wait_send()
+    for cc in range(2):
+        @pl.when(core != cc)
         def _():
-            acopy(j).wait_send()
+            acopy(0, cc).wait_send()
+    rcopy(wof.at[wo_rows, 0:768], wof.at[wo_rows, 0:768], ss_o.at[6], rs_o.at[6], sib).wait_send()
 
 
 def place_kernel(a_ref, b_ref, oa_ref, ob_ref):
@@ -510,14 +529,15 @@
             V((1280, 128), BF), V((8, 128), F32), V((768, 1536), BF), V((6, 512, 128), F32), V((512, 768), BF),
             V((256, 512), BF), V((1296, 768), F32), V((2, 96, 640), BF), V((1536, 640), BF), V((384, 1536), BF),
             V((2, 64, 640), BF), V((2, 2, 128, 640), BF), V((2, 1280, 64), BF), V((2, 1280, 256), F32),
-            V((128, 640), BF), V((640, 128), BF), V((128, 640), BF), V((80, 1024), BF), V((2, 80, 1536), BF),
-            V((80, 1536), BF), V((640, 1536), BF), V((1024, 1536), BF),
+            V((128, 640), BF), V((640, 128), BF), V((128, 640), BF), V((320, 512), BF), V((2, 160, 768), BF),
+            V((160, 768), BF), V((640, 1536), BF), V((512, 1536), BF),
+            V((160, 768), BF), V((160, 768), BF), V((160, 768), F32), V((2, 80, 768), BF), V((80, 768), BF),
             V((128, 1536), BF), V((6, 64, 384), BF), V((2, 64, 384), BF), V((6, 16, 384), BF), V((2, 4, 16, 384), BF),
             V((2, 16, 384), BF), V((64, 1536), BF), V((2, 192, 640), F32),
             V((80, 128), jnp.int32), V((512, 1536), BF), V((1, 96), F32), V((192, 1536), BF), V((12, 128), F32),
             pltpu.SemaphoreType.DMA((12,)),
-        ] + sems(15) + one + sems(9) + sems(6) + sems(6) + sems(2) + one + sems(6) + sems(8) + sems(4) + sems(12) + sems(2)
-        + sems(8) + sems(6) + sems(6) + sems(6) + sems(14),
+        ] + sems(15) + one + sems(9) + sems(6) + sems(6) + sems(2) + one + sems(6) + sems(8) + sems(4) + sems(7) + one + one
+        + sems(2) + sems(2) + sems(6) + sems(6) + sems(6) + sems(14),
         compiler_params=pltpu.CompilerParams(collective_id=0, has_side_effects=True, vmem_limit_bytes=56 << 20),
         name="layer",
     )(bases.reshape(80, 128), embed_w, conv_w.transpose(0, 2, 1).reshape(480, 1536), conv_b[None], qkv_w.T,

time: 83.5 us -> 77.3 us (0.926)
  Pallas kernels: 82.7 us -> 76.6 us
    pallas_call x1, Pallas kernels: 80.8 us -> 74.7 us  [per_device(): pl.pallas_call(layer_kernel, out_shape=(jax.ShapeDtypeStruct((80, 1536),...]
where the time goes in v4:
time: 77.3 us; the launch traced here: 77.2 us
  Pallas kernels  76.6 us (99%)
    pallas_call x1, Pallas kernels, per_device(): pl.pallas_call(layer_kernel, out_shape=(jax.ShapeDtypeStruct((80, 1536),...  74.7 us
    pallas_call x1, Pallas kernels, per_device(): pl.pallas_call(place_kernel, out_shape=(jax.ShapeDtypeStruct((80, 1536),...  1.82 us

profile of v4, /device:TPU:1, one launch (start us, length us, event | category | flops | bytes accessed | tf_op | source)
XLA Modules:
  0.0 77.2 jit_solution(13344703976502930307)
XLA Ops:
  0.6 74.7 %layer.1 = (bf16[80,1536]{1,0:T(8,128)(2,1)}, bf16[64,1536]{1,0:T(8,128)(2,1)}) custom-call(s32[80,128]{1,0:T(8,128)} %bitcast.12, bf16[512,1536]{1,0:T(8,128)(2,1)} %embed_hbm.1, bf16[480,1536]{1,0:T(8,128)(2,1)} %bitcast.9, f32[1,96]{1,0:T(1,128)} %bitcast.14, bf16[192,1536]{1,0:T(8,128)(2,1)} %bitcast.10, f32[12,128]{1,0:T(8,128)} %bitcast.13, ...), custom_call_target="tpu_custom_call" | custom-call | tf_op jit(solution)/shard_map/layer/pallas_call | solution.py:523
  75.4 1.8 %place.1 = (bf16[80,1536]{1,0:T(8,128)(2,1)}, bf16[64,1536]{1,0:T(8,128)(2,1)}) custom-call(bf16[80,1536]{1,0:T(8,128)(2,1)} %get-tuple-element.6.a_ref, bf16[64,1536]{1,0:T(8,128)(2,1)} %get-tuple-element.7.b_ref), custom_call_target="tpu_custom_call" | custom-call | tf_op jit(solution)/shard_map/place/pallas_call | solution.py:545

commit v5 on v4

--- a/solution.py
+++ b/solution.py
@@ -73,8 +73,6 @@
     greet = [(dp, lax.rem(me + d, 16)) for d in range(1, 16)]
     greet += [near(e) for e in (1, 2, 3)] + [far(e) for e in (1, 2, 3)] + [across(e) for e in range(4)]
     greet += [((1 - yh) * 16 + z, (1 - y) * 8 + lax.rem(me, 8))]
-    for to in greet:
-        pl.semaphore_signal(barrier, inc=1, device_id=to, device_id_type=MESH)
     loads = [
         pltpu.make_async_copy(src, dst, ld.at[i])
         for i, (src, dst) in enumerate(
@@ -86,6 +84,8 @@
     ]
     for cp in loads:
         cp.start()
+    for to in greet:
+        pl.semaphore_signal(barrier, inc=1, device_id=to, device_id_type=MESH)
     loads[0].wait()
     ball[pl.ds(_al(me * 80, 16), 80), :] = bases_ref[...].astype(F32).astype(BF)
     pl.semaphore_wait(barrier, len(greet))
@@ -196,32 +196,45 @@
 
     own_rows = pl.ds(_al(me * 96, 16), 96)
 
-    def s1(rel, ct):
+    pieces = (slice(0, LA), slice(LA, 640))
+
+    def s1(rel, ct, p):
         to = ctx(y, x + rel + 1, ct) if rel < 3 else ctx(1 - y, x, ct)
-        return rcopy(st.at[ct], xt.at[own_rows], ss1.at[rel * 2 + ct], rs1.at[rel * 2 + core], to)
+        lanes = pieces[p]
+        return rcopy(st.at[ct, :, lanes], xt.at[own_rows, lanes], ss1.at[(rel * 2 + ct) * 2 + p],
+                     rs1.at[(rel * 2 + core) * 2 + p], to)
+
+    def s1_sib(half, p):
+        lanes = pieces[p]
+        return rcopy(st.at[half, :, lanes], xt.at[own_rows, lanes], ss1.at[16 + p], rs1.at[16 + p], sib)
 
     for half in range(2):
-        lax.fori_loop(3 * half, 3 + 2 * half, taps, 0)
-        lax.fori_loop(5 * half, 5 * half + 5, act, 0)
-        for rel in (3, 0, 2):
-            cp = s1(rel, half)
-            cp.start()
-            sends.append(cp)
-
-        @pl.when(core == half)
-        def _():
-            xt[own_rows, :] = st[half]
-
-        @pl.when(core != half)
-        def _():
-            rcopy(st.at[half], xt.at[own_rows], ss1.at[8], rs1.at[8], sib).start()
+        for p, t0, t1, q0, q1 in (
+            (0, 3 * half, 2 + 2 * half, 5 * half, 5 * half + 2),
+            (1, 2 + 2 * half, 3 + 2 * half, 5 * half + 2, 5 * half + 5),
+        ):
+            lax.fori_loop(t0, t1, taps, 0)
+            lax.fori_loop(q0, q1, act, 0)
+            for rel in (3, 0, 2):
+                cp = s1(rel, half, p)
+                cp.start()
+                sends.append(cp)
+
+            @pl.when(core == half)
+            def _():
+                xt[own_rows, pieces[p]] = st[half, :, pieces[p]]
+
+            @pl.when(core != half)
+            def _():
+                s1_sib(half, p).start()
 
     def chip_rows(kk):
         return pl.ds(_al(kk * 192, 16), 192)
 
-    def s1_wait(rel):
+    def s1_wait(rel, p):
+        lanes = pieces[p]
         for cs in range(2):
-            rcopy(st.at[0], xt.at[own_rows], ss1.at[rel * 2 + cs], rs1.at[rel * 2 + cs], sib).wait_recv()
+            rcopy(st.at[0, :, lanes], xt.at[own_rows, lanes], ss1.at[0], rs1.at[(rel * 2 + cs) * 2 + p], sib).wait_recv()
 
     def chip_at(yy, d):
         return yy * 4 + lax.rem(x + d, 4)
@@ -237,15 +250,23 @@
     def half_rows(kk, i):
         return pl.ds(_al(kk * 192 + 96 * i, 16), 96)
 
-    s1_wait(3)
+    for i, d in ((0, 1), (1, 3)):
+        s1_wait(d - 1, 0)
+        to_y(d)
+        push(xt.at[half_rows(chip_at(y, 4 - d), i), pieces[0]], ss3.at[i], rs3.at[i], ctx(y, x + d, core))
+    s1_wait(3, 1)
     for d in (1, 3):
         push(xt.at[chip_rows(chip_at(1 - y, 0)), LA:640], ss2.at[2 + d], rs2.at[2 + d], ctx(y, x + d, core))
     for i, d in ((0, 1), (1, 3)):
-        s1_wait(d - 1)
-        to_y(d)
-        push(xt.at[half_rows(chip_at(y, 4 - d), i)], ss3.at[i], rs3.at[i], ctx(y, x + d, core))
-    for i in range(2):
-        rcopy(st.at[0], xt.at[own_rows], ss3.at[i], rs3.at[i], sib).wait_recv()
+        s1_wait(d - 1, 1)
+        push(xt.at[half_rows(chip_at(y, 4 - d), i), pieces[1]], ss3.at[2 + i], rs3.at[2 + i], ctx(y, x + d, core))
+
+    def s3_wait(p):
+        for i in range(2):
+            src = xt.at[own_rows, pieces[p]]
+            rcopy(src, src, ss3.at[0], rs3.at[2 * p + i], sib).wait_recv()
+
+    s3_wait(0)
     to_y(2)
     for i, d in ((0, 1), (1, 3)):
         src = xt.at[chip_rows(0), LA:640]
@@ -279,7 +300,10 @@
             sends.append(cp)
 
     wcopy.wait()
-    rcopy(st.at[0], xt.at[own_rows], ss1.at[8], rs1.at[8], sib).wait_recv()
+    for p in range(2):
+        s1_sib(0, p).wait_recv()
+    s3_wait(1)
+    s1_wait(3, 0)
 
     def sq(i, tot):
         v = xt[pl.ds(_al(i * 128, 128), 128), :].astype(F32)
@@ -449,49 +473,17 @@
     pcopy.start()
     pown[...] = _dot(aown[pl.ds(_al(y * 160, 16), 160), :], wof[:, core_cols])
 
-    for i in range(2):
-        for cp in fsend[i]:
-            cp.wait_recv()
-        acc = fr[i, 0].astype(F32)
-        for q in range(1, 4):
-            acc = acc + fr[i, q].astype(F32)
-        rc[i] = acc.astype(BF)
-        fcols = pl.ds(_al(yh * 768 + 384 * i, 128), 384)
-        fb[zrows, fcols] = rc[i]
-        for k, to in enumerate([across(e) for e in range(4)] + [near(e) for e in (1, 2, 3)]):
-            cp = rcopy(rc.at[i], fb.at[zrows, fcols], ss_g.at[7 * i + k], rs_g.at[7 * i + k], to)
-            cp.start()
-            gsend[i].append(cp)
-
-    @pl.when(core != y)
-    def _():
-        scopy.wait_recv()
-
-    pcopy.wait_recv()
-    whole = (sown[...].astype(F32) + (pown[...] + prx[...].astype(F32))).astype(BF)
-    obuf[0] = whole[0:80]
-    obuf[1] = whole[80:160]
-    ocopy = rcopy(obuf.at[1 - core], orx, ss_q, rs_q, sib)
-    ocopy.start()
-    out_ref[:, core_cols] = obuf[core]
-
-    for i in range(2):
-        for cp in gsend[i]:
-            cp.wait_recv()
-    grad_ref[...] = fb[...]
-    ocopy.wait_recv()
-    out_ref[:, pl.ds(_al(768 - core * 768, 128), 768)] = orx[...]
-
     @pl.when(core == y)
     def _():
         scopy.wait_send()
 
-    for cp in sends + bplane + bsib + cots + csib + [pcopy, ocopy]:
+    for cp in sends + bplane + bsib + cots + csib:
         cp.wait_send()
     for i in range(2):
-        for cp in ysend[i] + nsend[i] + fsend[i] + gsend[i]:
+        for cp in ysend[i] + nsend[i]:
             cp.wait_send()
-    rcopy(st.at[0], xt.at[own_rows], ss1.at[8], rs1.at[8], sib).wait_send()
+    for p in range(2):
+        s1_sib(0, p).wait_send()
     for cc in range(2):
         @pl.when(kx * 2 + cc != me)
         def _():
@@ -505,6 +497,45 @@
         def _():
             acopy(0, cc).wait_send()
     rcopy(wof.at[wo_rows, 0:768], wof.at[wo_rows, 0:768], ss_o.at[6], rs_o.at[6], sib).wait_send()
+
+    for i in range(2):
+        for cp in fsend[i]:
+            cp.wait_recv()
+        acc = fr[i, 0].astype(F32)
+        for q in range(1, 4):
+            acc = acc + fr[i, q].astype(F32)
+        rc[i] = acc.astype(BF)
+        fcols = pl.ds(_al(yh * 768 + 384 * i, 128), 384)
+        fb[zrows, fcols] = rc[i]
+        for k, to in enumerate([across(e) for e in range(4)] + [near(e) for e in (1, 2, 3)]):
+            cp = rcopy(rc.at[i], fb.at[zrows, fcols], ss_g.at[7 * i + k], rs_g.at[7 * i + k], to)
+            cp.start()
+            gsend[i].append(cp)
+
+    @pl.when(core != y)
+    def _():
+        scopy.wait_recv()
+
+    pcopy.wait_recv()
+    whole = (sown[...].astype(F32) + (pown[...] + prx[...].astype(F32))).astype(BF)
+    obuf[0] = whole[0:80]
+    obuf[1] = whole[80:160]
+    ocopy = rcopy(obuf.at[1 - core], orx, ss_q, rs_q, sib)
+    ocopy.start()
+    out_ref[:, core_cols] = obuf[core]
+
+    for i in range(2):
+        for cp in gsend[i]:
+            cp.wait_recv()
+    grad_ref[...] = fb[...]
+    ocopy.wait_recv()
+    out_ref[:, pl.ds(_al(768 - core * 768, 128), 768)] = orx[...]
+
+    for cp in [pcopy, ocopy]:
+        cp.wait_send()
+    for i in range(2):
+        for cp in fsend[i] + gsend[i]:
+            cp.wait_send()
 
 
 def place_kernel(a_ref, b_ref, oa_ref, ob_ref):
@@ -536,8 +567,8 @@
             V((2, 16, 384), BF), V((64, 1536), BF), V((2, 192, 640), F32),
             V((80, 128), jnp.int32), V((512, 1536), BF), V((1, 96), F32), V((192, 1536), BF), V((12, 128), F32),
             pltpu.SemaphoreType.DMA((12,)),
-        ] + sems(15) + one + sems(9) + sems(6) + sems(6) + sems(2) + one + sems(6) + sems(8) + sems(4) + sems(7) + one + one
-        + sems(2) + sems(2) + sems(6) + sems(6) + sems(6) + sems(14),
+        ] + sems(15) + one + sems(18) + sems(6) + sems(6) + sems(2) + one + sems(6) + sems(8) + sems(4) + sems(7) + one + one
+        + sems(4) + sems(2) + sems(6) + sems(6) + sems(6) + sems(14),
         compiler_params=pltpu.CompilerParams(collective_id=0, has_side_effects=True, vmem_limit_bytes=56 << 20),
         name="layer",
     )(bases.reshape(80, 128), embed_w, conv_w.transpose(0, 2, 1).reshape(480, 1536), conv_b[None], qkv_w.T,

time: 77.3 us -> 76 us (0.983)
  Pallas kernels: 76.6 us -> 74.9 us
    pallas_call x1, Pallas kernels: 74.7 us -> 73.1 us  [per_device(): pl.pallas_call(layer_kernel, out_shape=(jax.ShapeDtypeStruct((80, 1536),...]
where the time goes in v5:
time: 76 us; the launch traced here: 75.6 us
  Pallas kernels  74.9 us (99%)
    pallas_call x1, Pallas kernels, per_device(): pl.pallas_call(layer_kernel, out_shape=(jax.ShapeDtypeStruct((80, 1536),...  73.1 us
    pallas_call x1, Pallas kernels, per_device(): pl.pallas_call(place_kernel, out_shape=(jax.ShapeDtypeStruct((80, 1536),...  1.82 us

profile of v5, /device:TPU:1, one launch (start us, length us, event | category | flops | bytes accessed | tf_op | source)
XLA Modules:
  0.0 75.6 jit_solution(1849207730369854712)
XLA Ops:
  0.6 73.1 %layer.1 = (bf16[80,1536]{1,0:T(8,128)(2,1)}, bf16[64,1536]{1,0:T(8,128)(2,1)}) custom-call(s32[80,128]{1,0:T(8,128)} %bitcast.12, bf16[512,1536]{1,0:T(8,128)(2,1)} %embed_hbm.1, bf16[480,1536]{1,0:T(8,128)(2,1)} %bitcast.9, f32[1,96]{1,0:T(1,128)} %bitcast.14, bf16[192,1536]{1,0:T(8,128)(2,1)} %bitcast.10, f32[12,128]{1,0:T(8,128)} %bitcast.13, ...), custom_call_target="tpu_custom_call" | custom-call | tf_op jit(solution)/shard_map/layer/pallas_call | solution.py:554
  73.8 1.8 %place.1 = (bf16[80,1536]{1,0:T(8,128)(2,1)}, bf16[64,1536]{1,0:T(8,128)(2,1)}) custom-call(bf16[80,1536]{1,0:T(8,128)(2,1)} %get-tuple-element.6.a_ref, bf16[64,1536]{1,0:T(8,128)(2,1)} %get-tuple-element.7.b_ref), custom_call_target="tpu_custom_call" | custom-call | tf_op jit(solution)/shard_map/place/pallas_call | solution.py:576

commit v6 on v5

--- a/solution.py
+++ b/solution.py
@@ -121,16 +121,23 @@
         wc[2 * i + 1] = prod[:, 128:256]
         return c
 
-    lax.fori_loop(0, 2, comp, 0)
+    lax.fori_loop(0, 3, comp, 0)
+    for cp in loads[7:12]:
+        cp.wait()
+
+    for b in range(4):
+        for j in range(6):
+            wcp[128 * b : 128 * b + 128, 128 * j : 128 * j + 128] = wc[j, pl.ds(b, 128, stride=4), :].astype(BF)
+    yb[0:8, :] = jnp.zeros((8, 768), F32)
+    yb[1288:1296, :] = jnp.zeros((8, 768), F32)
+    bsc[...] = jnp.zeros((8, 128), F32)
+    bsc[0:1, 0:96] = convb_ref[...]
     for i, (dy, dx) in enumerate(plane):
         bplane[i].wait_recv()
         src = ball_of(ctx(ysel(dy), x + 4 - dx, core))
         cp = rcopy(src, src, ss_b.at[8 + i], rs_b.at[8 + i], sib)
         cp.start()
         bsib.append(cp)
-
-    for cp in loads[7:12]:
-        cp.wait()
 
     cots = []
 
@@ -146,30 +153,6 @@
     send_cot(3)
 
     sends = []
-    wrows = pl.ds(_al(core * 192, 16), 192)
-    for j in range(12):
-        cols = slice(128 * j, 128 * j + 128)
-        wt[wrows, cols] = (qkvt_ref[:, cols].astype(F32) * gain_ref[j : j + 1, :]).astype(BF)
-    wcopy = rcopy(wt.at[wrows], wt.at[wrows], ss_w, rs_w, sib)
-    wcopy.start()
-    for cc in range(2):
-        cols = slice(768 * cc, 768 * cc + 768)
-
-        @pl.when(core != cc)
-        def _():
-            rcopy(wof.at[wo_rows, cols], wof.at[wo_rows, cols], ss_o.at[6], rs_o.at[6], sib).start()
-
-    csib = [rcopy(cotr.at[my_tok], cotr.at[my_tok], ss_d.at[0], rs_d.at[0], sib)]
-    csib[0].start()
-
-    lax.fori_loop(2, 3, comp, 0)
-    for b in range(4):
-        for j in range(6):
-            wcp[128 * b : 128 * b + 128, 128 * j : 128 * j + 128] = wc[j, pl.ds(b, 128, stride=4), :].astype(BF)
-    yb[0:8, :] = jnp.zeros((8, 768), F32)
-    yb[1288:1296, :] = jnp.zeros((8, 768), F32)
-    bsc[...] = jnp.zeros((8, 128), F32)
-    bsc[0:1, 0:96] = convb_ref[...]
     for cp in bsib:
         cp.wait_recv()
 
@@ -228,6 +211,22 @@
             def _():
                 s1_sib(half, p).start()
 
+    wrows = pl.ds(_al(core * 192, 16), 192)
+    for j in range(12):
+        cols = slice(128 * j, 128 * j + 128)
+        wt[wrows, cols] = (qkvt_ref[:, cols].astype(F32) * gain_ref[j : j + 1, :]).astype(BF)
+    wcopy = rcopy(wt.at[wrows], wt.at[wrows], ss_w, rs_w, sib)
+    wcopy.start()
+    for cc in range(2):
+        cols = slice(768 * cc, 768 * cc + 768)
+
+        @pl.when(core != cc)
+        def _():
+            rcopy(wof.at[wo_rows, cols], wof.at[wo_rows, cols], ss_o.at[6], rs_o.at[6], sib).start()
+
+    csib = [rcopy(cotr.at[my_tok], cotr.at[my_tok], ss_d.at[0], rs_d.at[0], sib)]
+    csib[0].start()
+
     def chip_rows(kk):
         return pl.ds(_al(kk * 192, 16), 192)
 
@@ -292,13 +291,6 @@
         cp.start()
         cots.append(cp)
         cot_to_sib(d)
-    for d in (1, 3, 2):
-        for cc in range(2):
-            part = wof.at[wo_rows, 768 * cc : 768 * cc + 768]
-            cp = rcopy(part, part, ss_o.at[2 * d - 2 + cc], rs_o.at[2 * d - 2 + core], ctx(y, x + d, cc))
-            cp.start()
-            sends.append(cp)
-
     wcopy.wait()
     for p in range(2):
         s1_sib(0, p).wait_recv()
@@ -331,6 +323,13 @@
         kcopy.append(cp)
     for h in range(2):
         qt[h] = ((acc[h, 0:64] + part(h, 0, 64, 1 - y)) * scale * 0.125).astype(BF)
+
+    for d in (1, 3):
+        for cc in range(2):
+            part = wof.at[wo_rows, 768 * cc : 768 * cc + 768]
+            cp = rcopy(part, part, ss_o.at[2 * d - 2 + cc], rs_o.at[2 * d - 2 + core], ctx(y, x + d, cc))
+            cp.start()
+            sends.append(cp)
 
     scopy = rcopy(sbuf.at[1 - core], sown, ss_s, rs_s, sib)
 
@@ -395,16 +394,6 @@
                 @pl.when(kx * 2 + cc != me)
                 def _():
                     tcopy(t, cc).start()
-            an[a : a + w, :] = jnp.concatenate(outs, axis=0).T.astype(BF)
-
-    aown[a_rows, a_cols] = an[pl.ds(_al(x * 160, 16), 160), :]
-    for d in (1, 3, 2):
-        for cc in range(2):
-            acopy(d, cc).start()
-    for cc in range(2):
-        @pl.when(core != cc)
-        def _():
-            acopy(0, cc).start()
 
     for i in range(2):
         rcopy(cotr.at[my_tok, 0:768], cotr.at[my_tok, 0:768], ss_c.at[0], rs_c.at[2 + i], sib).wait_recv()
@@ -438,6 +427,28 @@
             cp = rcopy(gl.at[rows, cols], yr.at[k], ss_y.at[k], rs_y.at[k], ring_dev(e))
             cp.start()
             ysend[i].append(cp)
+
+    def o_wait(i):
+        rcopy(wof.at[0:64, 0:768], wof.at[0:64, 0:768], ss_o.at[0], rs_o.at[i], sib).wait_recv()
+
+    for i, d in ((0, 1), (1, 3)):
+        for cs in range(2):
+            o_wait(2 * d - 2 + cs)
+        part = wof.at[pl.ds(_al((lax.rem(x + 4 - d, 4) * 2 + i) * 64, 16), 64), core_cols]
+        cp = rcopy(part, part, ss_o.at[2 + i], rs_o.at[2 + i], ctx(y, x + d, core))
+        cp.start()
+        sends.append(cp)
+
+    an[...] = at[...].astype(F32).T.astype(BF)
+
+    aown[a_rows, a_cols] = an[pl.ds(_al(x * 160, 16), 160), :]
+    for d in (1, 3, 2):
+        for cc in range(2):
+            acopy(d, cc).start()
+    for cc in range(2):
+        @pl.when(core != cc)
+        def _():
+            acopy(0, cc).start()
 
     for i in range(2):
         rows, cols = block(ring, i)
@@ -463,8 +474,8 @@
             cp = rcopy(fr.at[i, za], fr.at[i, za], ss_f.at[k], rs_f.at[k], far(e))
             cp.start()
             fsend[i].append(cp)
-    for i in range(7):
-        rcopy(wof.at[0:64, 0:768], wof.at[0:64, 0:768], ss_o.at[0], rs_o.at[i], sib).wait_recv()
+    for i in (2, 3, 6):
+        o_wait(i)
     for i in range(2, 8):
         rcopy(an.at[0:160], aown.at[0:160, 0:128], ss_a.at[0], rs_a.at[i], sib).wait_recv()
     rcopy(an.at[0:160], aown.at[0:160, 0:128], ss_a.at[0], rs_a.at[1 - core], sib).wait_recv()

time: 76 us -> 75.7 us (level)
  no operation moved by 1% of the time
where the time goes in v6:
time: 75.7 us; the launch traced here: 75.5 us
  Pallas kernels  74.9 us (99%)
    pallas_call x1, Pallas kernels, per_device(): pl.pallas_call(layer_kernel, out_shape=(jax.ShapeDtypeStruct((80, 1536),...  73.1 us
    pallas_call x1, Pallas kernels, per_device(): pl.pallas_call(place_kernel, out_shape=(jax.ShapeDtypeStruct((80, 1536),...  1.82 us

profile of v6, /device:TPU:1, one launch (start us, length us, event | category | flops | bytes accessed | tf_op | source)
XLA Modules:
  0.0 75.5 jit_solution(1982001256492322655)
XLA Ops:
  0.6 73.1 %layer.1 = (bf16[80,1536]{1,0:T(8,128)(2,1)}, bf16[64,1536]{1,0:T(8,128)(2,1)}) custom-call(s32[80,128]{1,0:T(8,128)} %bitcast.12, bf16[512,1536]{1,0:T(8,128)(2,1)} %embed_hbm.1, bf16[480,1536]{1,0:T(8,128)(2,1)} %bitcast.9, f32[1,96]{1,0:T(1,128)} %bitcast.14, bf16[192,1536]{1,0:T(8,128)(2,1)} %bitcast.10, f32[12,128]{1,0:T(8,128)} %bitcast.13, ...), custom_call_target="tpu_custom_call" | custom-call | tf_op jit(solution)/shard_map/layer/pallas_call | solution.py:565
  73.7 1.8 %place.1 = (bf16[80,1536]{1,0:T(8,128)(2,1)}, bf16[64,1536]{1,0:T(8,128)(2,1)}) custom-call(bf16[80,1536]{1,0:T(8,128)(2,1)} %get-tuple-element.6.a_ref, bf16[64,1536]{1,0:T(8,128)(2,1)} %get-tuple-element.7.b_ref), custom_call_target="tpu_custom_call" | custom-call | tf_op jit(solution)/shard_map/place/pallas_call | solution.py:587
